TPU v7x, 512 devices: a whole 4x8x8 slice. The times are simulated.
512 devices in a mesh: src: 64 (over y, z), tgt: 8 (over x, core).
Axes of the slice: x: 4, y: 8, z: 8, core: 2. Of those that a mesh axis runs over, the one named last changes fastest.
Arguments:
- src_points: float32 [32, 24576], P(None, 'src'), may hold values from -14 to 14
- src_logw: float32 [24576], P('src'), may hold values from -1 to 1
- tgt_points: float32 [32, 131072], P(None, ('tgt', 'src')), may hold values from -6 to 6
- tgt_potential: float32 [1, 131072], P(None, ('tgt', 'src')), may hold values from -8 to 516
- tgt_logw: float32 [1, 131072], P(None, ('tgt', 'src')), may hold values from -1 to 1
Outputs:
- row_potential: float32 [24576], P('src')
- barycentre: float32 [32, 24576], P(None, 'src')
All inputs are finite; a program needn't handle non-finite values.
Results may differ from a plain program's by a relative error of at most 0.0003.
Values sent between devices are 32-bit elements; how exact they have to be, the bound alone decides.
A program may use at most 64 MiB of HBM per device.

v0:
```python
import math

import jax
import jax.numpy as jnp
from jax import lax
from jax.sharding import PartitionSpec as P

entropy_scale = 4.0


def tile_scores(xblock, yblock, gblock, lblock):
    half_source = 0.5 * jnp.sum(xblock * xblock, axis=0)
    half_target = 0.5 * jnp.sum(yblock * yblock, axis=0)
    inner_product = lax.dot_general(
        xblock,
        yblock,
        (((0,), (0,)), ((), ())),
        precision=lax.Precision.HIGHEST,
        preferred_element_type=jnp.float32,
    )
    transport = half_source[:, None] + half_target[None, :] - inner_product
    return (gblock[None, :] - transport) / entropy_scale + lblock[None, :]


def absorb_block(running, scores, yblock):
    row_peak, row_total, weighted = running
    new_peak = jnp.maximum(row_peak, jnp.max(scores, axis=1))
    rescale = jnp.exp(row_peak - new_peak)
    shares = jnp.exp(scores - new_peak[:, None])
    row_total = row_total * rescale + jnp.sum(shares, axis=1)
    weighted = weighted * rescale[None, :] + lax.dot_general(
        yblock,
        shares,
        (((1,), (1,)), ((), ())),
        precision=lax.Precision.HIGHEST,
        preferred_element_type=jnp.float32,
    )
    return (new_peak, row_total, weighted)


def on_device(src_points, src_logw, tgt_points, tgt_potential, tgt_logw):
    dims = src_points.shape[0]
    own_rows = src_points.shape[1]
    initial = (
        jnp.full((own_rows,), -jnp.inf, jnp.float32),
        jnp.zeros((own_rows,), jnp.float32),
        jnp.zeros((dims, own_rows), jnp.float32),
    )
    ypiece = lax.all_gather(tgt_points, "src", axis=1, tiled=True)
    gpiece = lax.all_gather(tgt_potential, "src", axis=1, tiled=True)
    lpiece = lax.all_gather(tgt_logw, "src", axis=1, tiled=True)
    columns = ypiece.shape[1]
    span_cols = math.gcd(columns, 2048)

    def advance(position, running_state):
        first_col = position * span_cols
        yblock = lax.dynamic_slice_in_dim(ypiece, first_col, span_cols, 1)
        gblock = lax.dynamic_slice_in_dim(gpiece[0], first_col, span_cols, 0)
        lblock = lax.dynamic_slice_in_dim(lpiece[0], first_col, span_cols, 0)
        return absorb_block(running_state, tile_scores(src_points, yblock, gblock, lblock), yblock)

    row_peak, row_total, weighted = lax.fori_loop(0, columns // span_cols, advance, initial)
    global_peak = lax.pmax(row_peak, "tgt")
    rescale = jnp.exp(row_peak - global_peak)
    row_total, weighted = lax.psum((row_total * rescale, weighted * rescale[None, :]), "tgt")
    row_potential = entropy_scale * src_logw - entropy_scale * (global_peak + jnp.log(row_total))
    return (row_potential, weighted / row_total[None, :])


def solution(mesh):
    return jax.shard_map(
        on_device,
        mesh=mesh,
        in_specs=(
            P(None, "src"),
            P("src"),
            P(None, ("tgt", "src")),
            P(None, ("tgt", "src")),
            P(None, ("tgt", "src")),
        ),
        out_specs=(P("src"), P(None, "src")),
        check_vma=False,
    )
```

profile of v0, /device:TPU:1, one launch (start us, length us, event | category | flops | bytes accessed | tf_op | source)
XLA Modules:
  0.0 227.9 jit_solution(17506766093940842379)
XLA Ops:
  7.2 0.0 all-gather.2.cloned.1.call-start
  7.2 0.7 all-gather.2.cloned.1.call-update
  7.9 45.1 %all_gather.9 = f32[1,16384]{1,0:T(1,128)S(1)} all-gather(f32[1,256]{1,0:T(1,128)} %param.10), channel_id=1, replica_groups=mesh['src'=64,'tgt'=8] {'src'}, dimensions={1}, use_global_device_ids=true | all-gather | bytes 66560 | tf_op jit(solution)/shard_map/all_gather | solution.py:50
  53.0 36.7 %all_gather.11 = f32[1,16384]{1,0:T(1,128)S(1)} all-gather(f32[1,256]{1,0:T(1,128)} %param.11), channel_id=1, replica_groups=mesh['src'=64,'tgt'=8] {'src'}, dimensions={1}, use_global_device_ids=true | all-gather | bytes 66560 | tf_op jit(solution)/shard_map/all_gather | solution.py:51
  89.7 0.8 multiply_reduce_fusion.1
  90.5 5.6 %all-gather.2.cloned.1.call-done = f32[32,16384]{1,0:T(8,128)} async-done(((f32[32,256]{1,0:T(8,128)}), f32[32,16384]{1,0:T(8,128)}) %all-gather.2.cloned.1.call-update) | async-done | bytes 2097168 | tf_op jit(solution)/shard_map/all_gather | solution.py:49
  96.1 0.0 copy-start
  96.1 72.4 %while.20 = (s32[]{:T(128)}, f32[384]{0:T(512)S(1)}, f32[384]{0:T(512)S(1)}, f32[32,384]{1,0:T(8,128)S(1)}, f32[1,16384]{1,0:T(1,128)S(1)}, /*index=5*/f32[384]{...) while((s32[]{:T(128)}, f32[384]{0:T(512)S(1)}, ...), condition=%wide.region_5.0_spmd.clone, body=%wide.region_1.5_spmd.clone.sunk | while | flops 611227904 | bytes 10482383 | solution.py:62
  96.1 1.0 multiply_reduce_fusion.3
  97.1 4.4 %fusion.23 = (f32[384]{0:T(512)S(1)}, f32[384,2048]{0,1:T(8,128)S(1)}) fusion(f32[2048]{0:T(1024)S(1)} %bitcast.17, f32[32,384]{1,0:T(8,128)} %get-tuple-element.361, f32[32,16384]{1,0:T(8,128)} %get-tuple-element.360, s32[]{:T(128)S(6)} %select_n.13, f32[2048]{0:T(1024)S(1)} %broadcast_multiply_fusion.5, f32[384]{0:T(512)S(1)} %broadcast_multiply_fusion.6, ...), kind=kOutput, calls=%fused_computation.29.clone.1 | convolution fusion | flops 306708096 | bytes 3484676 | tf_op jit(solution)/shard_map/while/body/eval_jaxpr/dot_general | solution.py:14
  101.6 0.5 fusion.24
  102.1 3.0 %fusion.26 = f32[32,384]{1,0:T(8,128)S(1)} fusion(f32[384,2048]{0,1:T(8,128)S(1)} %get-tuple-element.325, f32[384]{0:T(512)S(1)} %select_maximum_fusion.2, f32[32,16384]{1,0:T(8,128)} %get-tuple-element.360, s32[]{:T(128)S(6)} %select_n.13, f32[32,384]{1,0:T(8,128)S(1)} %get-tuple-element.344, f32[384]{0:T(512)S(1)} %get-tuple-element.327, ...), kind=kOutput, calls=%fused_computation.8.clone.1 | convolution fusion | flops 302813184 | bytes 3509253 | tf_op jit(solution)/shard_map/while/body/eval_jaxpr/dot_general | solution.py:31
  105.2 1.0 multiply_reduce_fusion.3
  106.2 4.4 %fusion.23 = (f32[384]{0:T(512)S(1)}, f32[384,2048]{0,1:T(8,128)S(1)}) fusion(f32[2048]{0:T(1024)S(1)} %bitcast.17, f32[32,384]{1,0:T(8,128)} %get-tuple-element.361, f32[32,16384]{1,0:T(8,128)} %get-tuple-element.360, s32[]{:T(128)S(6)} %select_n.13, f32[2048]{0:T(1024)S(1)} %broadcast_multiply_fusion.5, f32[384]{0:T(512)S(1)} %broadcast_multiply_fusion.6, ...), kind=kOutput, calls=%fused_computation.29.clone.1 | convolution fusion | flops 306708096 | bytes 3484676 | tf_op jit(solution)/shard_map/while/body/eval_jaxpr/dot_general | solution.py:14
  110.6 0.5 fusion.24
  111.2 3.0 %fusion.26 = f32[32,384]{1,0:T(8,128)S(1)} fusion(f32[384,2048]{0,1:T(8,128)S(1)} %get-tuple-element.325, f32[384]{0:T(512)S(1)} %select_maximum_fusion.2, f32[32,16384]{1,0:T(8,128)} %get-tuple-element.360, s32[]{:T(128)S(6)} %select_n.13, f32[32,384]{1,0:T(8,128)S(1)} %get-tuple-element.344, f32[384]{0:T(512)S(1)} %get-tuple-element.327, ...), kind=kOutput, calls=%fused_computation.8.clone.1 | convolution fusion | flops 302813184 | bytes 3509253 | tf_op jit(solution)/shard_map/while/body/eval_jaxpr/dot_general | solution.py:31
  114.2 1.0 multiply_reduce_fusion.3
  115.3 4.4 %fusion.23 = (f32[384]{0:T(512)S(1)}, f32[384,2048]{0,1:T(8,128)S(1)}) fusion(f32[2048]{0:T(1024)S(1)} %bitcast.17, f32[32,384]{1,0:T(8,128)} %get-tuple-element.361, f32[32,16384]{1,0:T(8,128)} %get-tuple-element.360, s32[]{:T(128)S(6)} %select_n.13, f32[2048]{0:T(1024)S(1)} %broadcast_multiply_fusion.5, f32[384]{0:T(512)S(1)} %broadcast_multiply_fusion.6, ...), kind=kOutput, calls=%fused_computation.29.clone.1 | convolution fusion | flops 306708096 | bytes 3484676 | tf_op jit(solution)/shard_map/while/body/eval_jaxpr/dot_general | solution.py:14
  119.7 0.5 fusion.24
  120.2 3.0 %fusion.26 = f32[32,384]{1,0:T(8,128)S(1)} fusion(f32[384,2048]{0,1:T(8,128)S(1)} %get-tuple-element.325, f32[384]{0:T(512)S(1)} %select_maximum_fusion.2, f32[32,16384]{1,0:T(8,128)} %get-tuple-element.360, s32[]{:T(128)S(6)} %select_n.13, f32[32,384]{1,0:T(8,128)S(1)} %get-tuple-element.344, f32[384]{0:T(512)S(1)} %get-tuple-element.327, ...), kind=kOutput, calls=%fused_computation.8.clone.1 | convolution fusion | flops 302813184 | bytes 3509253 | tf_op jit(solution)/shard_map/while/body/eval_jaxpr/dot_general | solution.py:31
  123.3 1.0 multiply_reduce_fusion.3
  124.3 4.4 %fusion.23 = (f32[384]{0:T(512)S(1)}, f32[384,2048]{0,1:T(8,128)S(1)}) fusion(f32[2048]{0:T(1024)S(1)} %bitcast.17, f32[32,384]{1,0:T(8,128)} %get-tuple-element.361, f32[32,16384]{1,0:T(8,128)} %get-tuple-element.360, s32[]{:T(128)S(6)} %select_n.13, f32[2048]{0:T(1024)S(1)} %broadcast_multiply_fusion.5, f32[384]{0:T(512)S(1)} %broadcast_multiply_fusion.6, ...), kind=kOutput, calls=%fused_computation.29.clone.1 | convolution fusion | flops 306708096 | bytes 3484676 | tf_op jit(solution)/shard_map/while/body/eval_jaxpr/dot_general | solution.py:14
  128.7 0.5 fusion.24
  129.3 3.0 %fusion.26 = f32[32,384]{1,0:T(8,128)S(1)} fusion(f32[384,2048]{0,1:T(8,128)S(1)} %get-tuple-element.325, f32[384]{0:T(512)S(1)} %select_maximum_fusion.2, f32[32,16384]{1,0:T(8,128)} %get-tuple-element.360, s32[]{:T(128)S(6)} %select_n.13, f32[32,384]{1,0:T(8,128)S(1)} %get-tuple-element.344, f32[384]{0:T(512)S(1)} %get-tuple-element.327, ...), kind=kOutput, calls=%fused_computation.8.clone.1 | convolution fusion | flops 302813184 | bytes 3509253 | tf_op jit(solution)/shard_map/while/body/eval_jaxpr/dot_general | solution.py:31
  132.3 1.0 multiply_reduce_fusion.3
  133.4 4.4 %fusion.23 = (f32[384]{0:T(512)S(1)}, f32[384,2048]{0,1:T(8,128)S(1)}) fusion(f32[2048]{0:T(1024)S(1)} %bitcast.17, f32[32,384]{1,0:T(8,128)} %get-tuple-element.361, f32[32,16384]{1,0:T(8,128)} %get-tuple-element.360, s32[]{:T(128)S(6)} %select_n.13, f32[2048]{0:T(1024)S(1)} %broadcast_multiply_fusion.5, f32[384]{0:T(512)S(1)} %broadcast_multiply_fusion.6, ...), kind=kOutput, calls=%fused_computation.29.clone.1 | convolution fusion | flops 306708096 | bytes 3484676 | tf_op jit(solution)/shard_map/while/body/eval_jaxpr/dot_general | solution.py:14
  137.8 0.5 fusion.24
  138.3 3.0 %fusion.26 = f32[32,384]{1,0:T(8,128)S(1)} fusion(f32[384,2048]{0,1:T(8,128)S(1)} %get-tuple-element.325, f32[384]{0:T(512)S(1)} %select_maximum_fusion.2, f32[32,16384]{1,0:T(8,128)} %get-tuple-element.360, s32[]{:T(128)S(6)} %select_n.13, f32[32,384]{1,0:T(8,128)S(1)} %get-tuple-element.344, f32[384]{0:T(512)S(1)} %get-tuple-element.327, ...), kind=kOutput, calls=%fused_computation.8.clone.1 | convolution fusion | flops 302813184 | bytes 3509253 | tf_op jit(solution)/shard_map/while/body/eval_jaxpr/dot_general | solution.py:31
  141.4 1.0 multiply_reduce_fusion.3
  142.4 4.4 %fusion.23 = (f32[384]{0:T(512)S(1)}, f32[384,2048]{0,1:T(8,128)S(1)}) fusion(f32[2048]{0:T(1024)S(1)} %bitcast.17, f32[32,384]{1,0:T(8,128)} %get-tuple-element.361, f32[32,16384]{1,0:T(8,128)} %get-tuple-element.360, s32[]{:T(128)S(6)} %select_n.13, f32[2048]{0:T(1024)S(1)} %broadcast_multiply_fusion.5, f32[384]{0:T(512)S(1)} %broadcast_multiply_fusion.6, ...), kind=kOutput, calls=%fused_computation.29.clone.1 | convolution fusion | flops 306708096 | bytes 3484676 | tf_op jit(solution)/shard_map/while/body/eval_jaxpr/dot_general | solution.py:14
  146.8 0.5 fusion.24
  147.4 3.0 %fusion.26 = f32[32,384]{1,0:T(8,128)S(1)} fusion(f32[384,2048]{0,1:T(8,128)S(1)} %get-tuple-element.325, f32[384]{0:T(512)S(1)} %select_maximum_fusion.2, f32[32,16384]{1,0:T(8,128)} %get-tuple-element.360, s32[]{:T(128)S(6)} %select_n.13, f32[32,384]{1,0:T(8,128)S(1)} %get-tuple-element.344, f32[384]{0:T(512)S(1)} %get-tuple-element.327, ...), kind=kOutput, calls=%fused_computation.8.clone.1 | convolution fusion | flops 302813184 | bytes 3509253 | tf_op jit(solution)/shard_map/while/body/eval_jaxpr/dot_general | solution.py:31
  150.4 1.0 multiply_reduce_fusion.3
  151.5 4.4 %fusion.23 = (f32[384]{0:T(512)S(1)}, f32[384,2048]{0,1:T(8,128)S(1)}) fusion(f32[2048]{0:T(1024)S(1)} %bitcast.17, f32[32,384]{1,0:T(8,128)} %get-tuple-element.361, f32[32,16384]{1,0:T(8,128)} %get-tuple-element.360, s32[]{:T(128)S(6)} %select_n.13, f32[2048]{0:T(1024)S(1)} %broadcast_multiply_fusion.5, f32[384]{0:T(512)S(1)} %broadcast_multiply_fusion.6, ...), kind=kOutput, calls=%fused_computation.29.clone.1 | convolution fusion | flops 306708096 | bytes 3484676 | tf_op jit(solution)/shard_map/while/body/eval_jaxpr/dot_general | solution.py:14
  155.9 0.5 fusion.24
  156.4 3.0 %fusion.26 = f32[32,384]{1,0:T(8,128)S(1)} fusion(f32[384,2048]{0,1:T(8,128)S(1)} %get-tuple-element.325, f32[384]{0:T(512)S(1)} %select_maximum_fusion.2, f32[32,16384]{1,0:T(8,128)} %get-tuple-element.360, s32[]{:T(128)S(6)} %select_n.13, f32[32,384]{1,0:T(8,128)S(1)} %get-tuple-element.344, f32[384]{0:T(512)S(1)} %get-tuple-element.327, ...), kind=kOutput, calls=%fused_computation.8.clone.1 | convolution fusion | flops 302813184 | bytes 3509253 | tf_op jit(solution)/shard_map/while/body/eval_jaxpr/dot_general | solution.py:31
  159.5 1.0 multiply_reduce_fusion.3
  160.5 4.4 %fusion.23 = (f32[384]{0:T(512)S(1)}, f32[384,2048]{0,1:T(8,128)S(1)}) fusion(f32[2048]{0:T(1024)S(1)} %bitcast.17, f32[32,384]{1,0:T(8,128)} %get-tuple-element.361, f32[32,16384]{1,0:T(8,128)} %get-tuple-element.360, s32[]{:T(128)S(6)} %select_n.13, f32[2048]{0:T(1024)S(1)} %broadcast_multiply_fusion.5, f32[384]{0:T(512)S(1)} %broadcast_multiply_fusion.6, ...), kind=kOutput, calls=%fused_computation.29.clone.1 | convolution fusion | flops 306708096 | bytes 3484676 | tf_op jit(solution)/shard_map/while/body/eval_jaxpr/dot_general | solution.py:14
  164.9 0.5 fusion.24
  165.5 3.0 %fusion.26 = f32[32,384]{1,0:T(8,128)S(1)} fusion(f32[384,2048]{0,1:T(8,128)S(1)} %get-tuple-element.325, f32[384]{0:T(512)S(1)} %select_maximum_fusion.2, f32[32,16384]{1,0:T(8,128)} %get-tuple-element.360, s32[]{:T(128)S(6)} %select_n.13, f32[32,384]{1,0:T(8,128)S(1)} %get-tuple-element.344, f32[384]{0:T(512)S(1)} %get-tuple-element.327, ...), kind=kOutput, calls=%fused_computation.8.clone.1 | convolution fusion | flops 302813184 | bytes 3509253 | tf_op jit(solution)/shard_map/while/body/eval_jaxpr/dot_general | solution.py:31
  168.5 29.8 %pmax.7 = f32[384]{0:T(512)S(1)} all-reduce(f32[384]{0:T(512)S(1)} %get-tuple-element.200), channel_id=1, replica_groups=mesh['src'=64,'tgt'=8] {'tgt'}, use_global_device_ids=true, to_apply=%region_6.0 | all-reduce | flops 384 | bytes 3072 | tf_op jit(solution)/shard_map/pmax | solution.py:63
  198.4 21.4 %all-reduce = (f32[384]{0:T(512)S(1)}, f32[32,384]{1,0:T(8,128)S(1)}) all-reduce(f32[384]{0:T(512)S(1)} %get-tuple-element.255, f32[32,384]{1,0:T(8,128)S(1)} %broadcast_multiply_fusion.2), channel_id=1, replica_groups=mesh['src'=64,'tgt'=8] {'tgt'}, use_global_device_ids=true, to_apply=%region_7.0 | all-reduce | flops 12672 | bytes 101376 | tf_op jit(solution)/shard_map/psum | solution.py:65
  219.8 0.6 broadcast_divide_fusion
  220.4 0.0 copy-done
  220.4 0.6 multiply_subtract_fusion
  (53 shorter events, 0.4 us)
Async XLA Ops:
  7.2 88.9 %all-gather.2.cloned.1.call-start = ((), (), s32[]{:S(2)}) async-start(), calls=%async_computation | async-start | bytes 2129920 | tf_op jit(solution)/shard_map/all_gather | solution.py:49
  96.1 124.3 %copy-start = (f32[384]{0:T(512)S(1)}, f32[384]{0:T(512)}, u32[]{:S(2)}) copy-start(f32[384]{0:T(512)} %param.8) | copy-start | bytes 4612
Sparse Core Ops, SparseCore 0:
  11.0 85.0 all-gather.1
where the time goes:
time: 230 us; the launch traced here: 228 us
  blocking collectives  133 us (58%)
  matrix products  59.2 us (26%)
  other arithmetic  14.6 us (6%)
  between operations  14.1 us (6%)
  waiting for transfers between devices  6.28 us (3%)
    all_gather x1, blocking collectives, on_device(): gpiece = lax.all_gather(tgt_potential, 'src', axis=1, tiled=True)  45.1 us
    all_gather x1, blocking collectives, on_device(): lpiece = lax.all_gather(tgt_logw, 'src', axis=1, tiled=True)  36.7 us
    dot_general x8, matrix products, tile_scores(): lax.dot_general(xblock, yblock, (((0,), (0,)), ((), ())), precision=lax.P...  35.2 us
    pmax x1, blocking collectives, on_device(): global_peak = lax.pmax(row_peak, 'tgt')  29.8 us
    dot_general x8, matrix products, absorb_block(): lax.dot_general(yblock, shares, (((1,), (1,)), ((), ())), precision=lax.P...  24 us
    psum x1, blocking collectives, on_device(): lax.psum((row_total * rescale, weighted * rescale[None, :]), 'tgt')  21.4 us
    reduce_sum x8, other arithmetic, tile_scores(): half_target = 0.5 * jnp.sum(yblock * yblock, axis=0)  7.93 us
    all_gather x1, waiting for transfers between devices, on_device(): ypiece = lax.all_gather(tgt_points, 'src', axis=1, tiled=True)  5.6 us
  transfers between devices with their start and end apart: 1, of which 1 were waited for; matrix products, arithmetic and copies ran while one was open for 0% of the time, Pallas kernels for 0%

commit v1 on v0

v1 whole, which is shorter than its diff:
```python
import functools
import math

import jax
import jax.numpy as jnp
from jax import lax
from jax.experimental import pallas as pl
from jax.experimental.pallas import tpu as pltpu
from jax.sharding import PartitionSpec as P

ENTROPY = 4.0
LOG2E = math.log2(math.e)
LN2 = math.log(2.0)
MESH = pl.DeviceIdType.MESH
BF16, F32 = jnp.bfloat16, jnp.float32

NY, NZ, NX, CORES = 8, 8, 4, 2
DIMS, ROWS, COLS = 32, 384, 256
TILE = 256
GROUP = 4
SHARDS = NY * CORES
BLOCKS = NZ // CORES
SPAN = GROUP * COLS
TILES = BLOCKS * ROWS // TILE
DEPTH = 256
LANES = 128
COL_TALL = 72
ROW_TALL = 104

DIRECT = {0: 0, 1: 2, 7: 3, 2: 6, 6: 7, 3: 10, 5: 11, 4: 14}
PASSED = {0: 1, 1: 4, 7: 5, 2: 8, 6: 9, 3: 12, 5: 13, 4: 15}
NEAR_FIRST = (1, 7, 2, 6, 3, 5, 4)
EVEN = (4, 2, 6, 0)
ODD = (3, 5, 1, 7)


def split(value):
    first = value.astype(BF16)
    rest = value - first.astype(F32)
    second = rest.astype(BF16)
    third = (rest - second.astype(F32)).astype(BF16)
    return first, second, third


def kernel(
    x_hbm, y_hbm, g_hbm, l_hbm, pot_ref, bary_ref,
    xown, yown, gown, lown, xraw, craw, ya, yw, xa, s0, s1, m0, m1, mrun, acc, pout, pin, xin,
    in_sem, crecv, csend, fsend, rrecv, rsend, precv, psend, xrecv, xsend,
):
    src, tgt = lax.axis_index("src"), lax.axis_index("tgt")
    yi, zi = src // NZ, src % NZ
    xi, core = tgt // CORES, tgt % CORES
    odd = (zi + core) % 2
    home = odd == 0

    def y_peer(e):
        return (((yi + e) % NY) * NZ + zi, tgt)

    def z_peer(e):
        return (yi * NZ + (zi + e) % NZ, tgt)

    def t_peer(e):
        return (src, (tgt + e) % (NX * CORES))

    sibling = (src, xi * CORES + 1 - core)

    barrier = pltpu.get_barrier_semaphore()
    for e in range(1, 8):
        pl.semaphore_signal(barrier, inc=1, device_id=y_peer(e), device_id_type=MESH)
        pl.semaphore_signal(barrier, inc=1, device_id=z_peer(e), device_id_type=MESH)
        pl.semaphore_signal(barrier, inc=1, device_id=t_peer(e), device_id_type=MESH)

    loads = [
        pltpu.make_async_copy(a, b, in_sem.at[i])
        for i, (a, b) in enumerate(((x_hbm, xown), (y_hbm, yown), (g_hbm, gown), (l_hbm, lown)))
    ]
    for load in loads:
        load.start()
    mrun[...] = jnp.full_like(mrun, -1e30)
    acc[...] = jnp.zeros_like(acc)
    for load in loads:
        load.wait()

    y = yown[...]
    bias = (gown[...] - 0.5 * jnp.sum(y * y, axis=0, keepdims=True)) * (LOG2E / ENTROPY) + lown[...] * LOG2E
    for half in range(2):
        lanes = slice(half * LANES, (half + 1) * LANES)
        craw[0, half * DIMS : (half + 1) * DIMS, :] = y[:, lanes]
    craw[0, 64:72, :] = jnp.concatenate(
        [bias[:, :LANES], bias[:, LANES:], jnp.zeros((6, LANES), F32)], axis=0
    )

    pl.semaphore_wait(barrier, 21)

    def column_copy(e):
        place = DIRECT[(8 - e) % 8]
        return pltpu.make_async_remote_copy(
            src_ref=craw.at[0], dst_ref=craw.at[place], send_sem=csend.at[e], recv_sem=crecv.at[place],
            device_id=y_peer(e), device_id_type=MESH,
        )

    def pass_copy(e):
        return pltpu.make_async_remote_copy(
            src_ref=craw.at[DIRECT[e]], dst_ref=craw.at[PASSED[e]], send_sem=fsend.at[e],
            recv_sem=crecv.at[PASSED[e]], device_id=sibling, device_id_type=MESH,
        )

    def row_copy(e):
        back = (8 - e) % 8
        slot = EVEN.index(back) if back % 2 == 0 else ODD.index(back)
        return pltpu.make_async_remote_copy(
            src_ref=xown, dst_ref=xraw.at[slot], send_sem=rsend.at[e], recv_sem=rrecv.at[slot],
            device_id=z_peer(e), device_id_type=MESH,
        )

    pass_copy(0).start()
    for e in NEAR_FIRST:
        column_copy(e).start()

    @pl.when(home)
    def _():
        for e in NEAR_FIRST:
            row_copy(e).start()

    def wait_column(place):
        pltpu.make_async_remote_copy(
            src_ref=craw.at[place], dst_ref=craw.at[place], send_sem=csend.at[0], recv_sem=crecv.at[place],
            device_id=sibling, device_id_type=MESH,
        ).wait_recv()

    def wait_rows(slot):
        pltpu.make_async_remote_copy(
            src_ref=xraw.at[slot], dst_ref=xraw.at[slot], send_sem=rsend.at[0], recv_sem=rrecv.at[slot],
            device_id=sibling, device_id_type=MESH,
        ).wait_recv()

    def prepare_rows(slot):
        x1, x2, x3 = split(xraw[slot] * (LOG2E / ENTROPY))
        row = lax.broadcasted_iota(jnp.int32, (64, ROWS), 0)
        ones = jnp.where(row < 3, 1.0, 0.0).astype(BF16)
        xa[:, slot * ROWS : (slot + 1) * ROWS] = jnp.concatenate([x1, x1, x2, x2, x1, x3, ones], axis=0)

    def prepare_columns(place):
        raw = craw[place]
        y1, y2, y3 = split(jnp.concatenate([raw[:32], raw[32:64]], axis=1))
        b = jnp.concatenate([raw[64:65], raw[65:66]], axis=1)
        b1 = b.astype(BF16).astype(F32)
        b2 = (b - b1).astype(BF16).astype(F32)
        b3 = b - b1 - b2
        row = lax.broadcasted_iota(jnp.int32, (64, COLS), 0)
        biases = jnp.where(row == 0, b1, jnp.where(row == 1, b2, jnp.where(row == 2, b3, 0.0))).astype(BF16)
        deep = jnp.concatenate([y1, y2, y1, y2, y3, y1, biases], axis=0)
        first = place * COLS if isinstance(place, int) else pl.multiple_of(place * COLS, COLS)
        ya[pl.ds(first, COLS), :] = deep.T
        yw[:, pl.ds(first, COLS)] = jnp.concatenate([y1, jnp.ones((16, COLS), BF16), y2], axis=0)

    def tile_lanes(tile):
        return pl.ds(pl.multiple_of(tile * TILE, TILE), TILE)

    def scores(group, tile, s, m):
        first = pl.multiple_of(group * SPAN, SPAN)
        value = jnp.dot(ya[pl.ds(first, SPAN), :], xa[:, tile_lanes(tile)], preferred_element_type=F32)
        s[...] = value
        m[...] = jnp.max(value.reshape(SPAN // 8, 8, TILE), axis=0)

    def absorb(group, tile, s, m):
        first = pl.multiple_of(group * SPAN, SPAN)
        lanes = tile_lanes(tile)
        old = mrun[0:1, lanes]
        new = jnp.maximum(old, jnp.max(m[...], axis=0, keepdims=True))
        mrun[0:1, lanes] = new
        share = jnp.exp2(s[...] - new)
        high = share.astype(BF16)
        low = (share - high.astype(F32)).astype(BF16)
        sums = jnp.dot(yw[:, pl.ds(first, SPAN)], high, preferred_element_type=F32)
        rest = jnp.dot(yw[0:48, pl.ds(first, SPAN)], low, preferred_element_type=F32)
        sums = jnp.concatenate([sums[:48] + rest, sums[48:]], axis=0)
        acc[:, lanes] = acc[:, lanes] * jnp.exp2(old - new) + sums

    def tile_at(step):
        group, place = step // TILES, step % TILES
        return group, jnp.where(group == 0, TILES - 1 - place, place)

    def block_offset(block):
        return EVEN[block] + odd * (ODD[block] - EVEN[block])

    def partial_copy(block):
        offset = block_offset(block)
        place = (NZ - offset) % NZ
        return pltpu.make_async_remote_copy(
            src_ref=pout.at[block], dst_ref=pin.at[place], send_sem=psend.at[block], recv_sem=precv.at[place],
            device_id=z_peer(offset), device_id_type=MESH,
        )

    def put_partial(ref, index, weighted, totals, peaks):
        for third in range(3):
            ref[index, third * DIMS : (third + 1) * DIMS, :] = weighted[third]
        ref[index, 96:104, :] = jnp.concatenate([*totals, *peaks, jnp.zeros((2, LANES), F32)], axis=0)

    def finish_block(block):
        weighted, totals, peaks = [], [], []
        for third in range(3):
            lanes = slice(block * ROWS + third * LANES, block * ROWS + (third + 1) * LANES)
            weighted.append(acc[0:32, lanes] + acc[48:80, lanes])
            totals.append(acc[32:33, lanes])
            peaks.append(mrun[0:1, lanes])
        if block < 3:
            put_partial(pout, block, weighted, totals, peaks)
            partial_copy(block).start()
        else:

            @pl.when(home)
            def _():
                put_partial(pin, 0, weighted, totals, peaks)

            @pl.when(jnp.logical_not(home))
            def _():
                put_partial(pout, block, weighted, totals, peaks)
                partial_copy(block).start()

    @pl.when(home)
    def _():
        xraw[3] = xown[...]

    @pl.when(jnp.logical_not(home))
    def _():
        wait_rows(3)

    prepare_rows(3)
    prepare_columns(0)
    wait_column(1)
    prepare_columns(1)
    for e in (1, 7):
        wait_column(DIRECT[e])
        pass_copy(e).start()
    for e in (1, 7):
        prepare_columns(DIRECT[e])
    wait_rows(2)
    prepare_rows(2)
    scores(0, TILES - 1, s0, m0)

    last = SHARDS // GROUP * TILES - 1

    def two_steps(turn, carry):
        group, third = turn // 3, turn % 3

        @pl.when(turn == 1)
        def _():
            for slot in (1, 0):
                wait_rows(slot)
                prepare_rows(slot)

        for when, passed in ((1, (2, 6)), (4, (3, 5)), (7, (4,))):

            @pl.when(turn == when)
            def _(passed=passed):
                for e in passed:
                    wait_column(DIRECT[e])
                    pass_copy(e).start()

        for when, arrived in ((2, (4, 5)), (5, (8, 9)), (8, (12, 13, 15))):

            @pl.when(turn == when)
            def _(arrived=arrived):
                for place in arrived:
                    wait_column(place)

        @pl.when(jnp.logical_and(third == 2, group < 3))
        def _():
            for place in range(GROUP):
                prepare_columns((group + 1) * GROUP + place)

        step = turn * 2
        for half, (now, now_m, later, later_m) in enumerate(((s0, m0, s1, m1), (s1, m1, s0, m0))):
            g_now, t_now = tile_at(step + half)
            g_next, t_next = tile_at(jnp.minimum(step + half + 1, last))
            scores(g_next, t_next, later, later_m)
            absorb(g_now, t_now, now, now_m)

        for when, block in ((9, 0), (10, 1)):

            @pl.when(turn == when)
            def _(block=block):
                finish_block(block)

        return carry

    lax.fori_loop(0, 12, two_steps, 0)
    finish_block(2)
    finish_block(3)

    def merge(ref, places):
        tops = [ref[place, 96:104, :] for place in places]
        peak = functools.reduce(jnp.maximum, tops)[3:6]
        factors = [jnp.exp2(top[3:6] - peak) for top in tops]
        total = functools.reduce(jnp.add, [top[0:3] * f for top, f in zip(tops, factors, strict=True)])
        weighted = []
        for third in range(3):
            rows = slice(third * DIMS, (third + 1) * DIMS)
            terms = [ref[place, rows, :] * f[third : third + 1] for place, f in zip(places, factors, strict=True)]
            weighted.append(functools.reduce(jnp.add, terms))
        return weighted, total, peak

    def sum_copy(e):
        return pltpu.make_async_remote_copy(
            src_ref=xin.at[xi], dst_ref=xin.at[xi], send_sem=xsend.at[e], recv_sem=xrecv.at[xi],
            device_id=t_peer(e), device_id_type=MESH,
        )

    def wait_sum(place):
        pltpu.make_async_remote_copy(
            src_ref=xin.at[place], dst_ref=xin.at[place], send_sem=xsend.at[0], recv_sem=xrecv.at[place],
            device_id=sibling, device_id_type=MESH,
        ).wait_recv()

    @pl.when(home)
    def _():
        for place in range(1, NZ):
            pltpu.make_async_remote_copy(
                src_ref=pin.at[place], dst_ref=pin.at[place], send_sem=psend.at[0], recv_sem=precv.at[place],
                device_id=sibling, device_id_type=MESH,
            ).wait_recv()
        weighted, total, peak = merge(pin, range(NZ))
        put_partial(xin, xi, weighted, [total], [peak])
        for e in range(1, 8):
            sum_copy(e).start()

    for place in range(1, NX):
        wait_sum((xi + place) % NX)

    @pl.when(jnp.logical_not(home))
    def _():
        wait_sum(xi)

    weighted, total, peak = merge(xin, range(NX))
    x = xown[...]
    norm = 0.5 * jnp.sum(x * x, axis=0, keepdims=True)
    for third in range(3):
        lanes = slice(third * LANES, (third + 1) * LANES)
        bary_ref[:, lanes] = weighted[third] / total[third : third + 1]
        logs = peak[third : third + 1] * LN2 + jnp.log(total[third : third + 1])
        pot_ref[:, lanes] = norm[:, lanes] - ENTROPY * logs

    for e in range(1, 8):
        column_copy(e).wait_send()
    for e in range(8):
        pass_copy(e).wait_send()
    for block in range(3):
        partial_copy(block).wait_send()

    @pl.when(home)
    def _():
        for e in range(1, 8):
            row_copy(e).wait_send()
            sum_copy(e).wait_send()

    @pl.when(jnp.logical_not(home))
    def _():
        partial_copy(3).wait_send()


def on_device(src_points, src_logw, tgt_points, tgt_potential, tgt_logw):
    dma = pltpu.SemaphoreType.DMA
    vmem = pltpu.VMEM
    potential, barycentre = pl.pallas_call(
        kernel,
        out_shape=(jax.ShapeDtypeStruct((1, ROWS), F32), jax.ShapeDtypeStruct((DIMS, ROWS), F32)),
        in_specs=[pl.BlockSpec(memory_space=pl.ANY)] * 4,
        out_specs=(pl.BlockSpec(memory_space=pltpu.VMEM),) * 2,
        scratch_shapes=[
            vmem((DIMS, ROWS), F32),
            vmem((DIMS, COLS), F32),
            vmem((1, COLS), F32),
            vmem((1, COLS), F32),
            vmem((BLOCKS, DIMS, ROWS), F32),
            vmem((SHARDS, COL_TALL, LANES), F32),
            vmem((SHARDS * COLS, DEPTH), BF16),
            vmem((80, SHARDS * COLS), BF16),
            vmem((DEPTH, BLOCKS * ROWS), BF16),
            vmem((SPAN, TILE), F32),
            vmem((SPAN, TILE), F32),
            vmem((8, TILE), F32),
            vmem((8, TILE), F32),
            vmem((8, BLOCKS * ROWS), F32),
            vmem((80, BLOCKS * ROWS), F32),
            vmem((BLOCKS, ROW_TALL, LANES), F32),
            vmem((NZ, ROW_TALL, LANES), F32),
            vmem((NX, ROW_TALL, LANES), F32),
            dma((4,)),
            dma((SHARDS,)),
            dma((8,)),
            dma((8,)),
            dma((BLOCKS,)),
            dma((8,)),
            dma((NZ,)),
            dma((BLOCKS,)),
            dma((NX,)),
            dma((8,)),
        ],
        compiler_params=pltpu.CompilerParams(
            collective_id=0, has_side_effects=True, vmem_limit_bytes=40 * 2**20
        ),
    )(src_points, tgt_points, tgt_potential, tgt_logw)
    return ENTROPY * src_logw + potential[0], barycentre


def solution(mesh):
    return jax.shard_map(
        on_device,
        mesh=mesh,
        in_specs=(
            P(None, "src"),
            P("src"),
            P(None, ("tgt", "src")),
            P(None, ("tgt", "src")),
            P(None, ("tgt", "src")),
        ),
        out_specs=(P("src"), P(None, "src")),
        check_vma=False,
    )
```

time: 230 us -> 52.4 us (0.23)
  blocking collectives: 133 us -> 0 us
  matrix products: 59.2 us -> 0 us
  Pallas kernels: 0 us -> 46.7 us
  other arithmetic: 14.6 us -> 0.6 us
  between operations: 14.1 us -> 0.66 us
  waiting for transfers between devices: 6.28 us -> 0 us
  local copies, waits for them, and re-layouts: 0.11 us -> 4.18 us
    all_gather x2 -> x0, blocking collectives: 81.8 us -> none  [the longest x1 45.1 us: on_device(): gpiece = lax.all_gather(tgt_potential, 'src', axis=1, tiled=True)]
    dot_general x16 -> x0, matrix products: 59.2 us -> none  [the longest x8 35.2 us: tile_scores(): lax.dot_general(xblock, yblock, (((0,), (0,)), ((), ())), precision=lax.P...]
    pallas_call x0 -> x1, Pallas kernels: none -> 46.7 us  [on_device(): pl.pallas_call(kernel, out_shape=(jax.ShapeDtypeStruct((1, ROWS), F32), j...]
    pmax x1 -> x0, blocking collectives: 29.8 us -> none  [on_device(): global_peak = lax.pmax(row_peak, 'tgt')]
    psum x1 -> x0, blocking collectives: 21.4 us -> none  [on_device(): lax.psum((row_total * rescale, weighted * rescale[None, :]), 'tgt')]
    reduce_sum x17 -> x0, other arithmetic: 13.1 us -> none  [the longest x8 7.93 us: tile_scores(): half_target = 0.5 * jnp.sum(yblock * yblock, axis=0)]
    all_gather x1 -> x0, waiting for transfers between devices: 5.6 us -> none  [on_device(): ypiece = lax.all_gather(tgt_points, 'src', axis=1, tiled=True)]
    unnamed x2 -> x11, local copies, waits for them, and re-layouts: 0.01 us -> 4.18 us
  transfers between devices with their start and end apart: 1 -> 0, of which waited for: 1 -> 0; matrix products, arithmetic and copies ran while one was open for 0% -> 0% of each run, Pallas kernels for 0% -> 0%
where the time goes in v1:
time: 52.4 us; the launch traced here: 52.1 us
  Pallas kernels  46.7 us (89%)
  local copies, waits for them, and re-layouts  4.18 us (8%)
  between operations  0.66 us (1%)
  other arithmetic  0.6 us (1%)
    pallas_call x1, Pallas kernels, on_device(): pl.pallas_call(kernel, out_shape=(jax.ShapeDtypeStruct((1, ROWS), F32), j...  46.7 us
    unnamed x11, local copies, waits for them, and re-layouts  4.18 us

profile of v1, /device:TPU:1, one launch (start us, length us, event | category | flops | bytes accessed | tf_op | source)
XLA Modules:
  0.0 52.1 jit_solution(2160608294325728989)
XLA Ops:
  0.6 0.0 copy-start
  0.6 0.8 %copy-done = f32[32,384]{1,0:T(8,128)S(1)} copy-done((f32[32,384]{1,0:T(8,128)S(1)}, f32[32,384]{1,0:T(8,128)}, u32[]{:S(2)}) %copy-start) | copy-done | bytes 49176
  1.4 0.0 copy-start.1
  1.4 0.8 %copy-done.1 = f32[32,256]{1,0:T(8,128)S(1)} copy-done((f32[32,256]{1,0:T(8,128)S(1)}, f32[32,256]{1,0:T(8,128)}, u32[]{:S(2)}) %copy-start.1) | copy-done | bytes 32792
  2.2 0.0 copy-start.2
  2.2 0.7 %copy-done.2 = f32[1,256]{1,0:T(1,128)S(1)} copy-done((f32[1,256]{1,0:T(1,128)S(1)}, f32[1,256]{1,0:T(1,128)}, u32[]{:S(2)}) %copy-start.2) | copy-done | bytes 1048
  2.9 0.0 copy-start.3
  2.9 0.7 %copy-done.3 = f32[1,256]{1,0:T(1,128)S(1)} copy-done((f32[1,256]{1,0:T(1,128)S(1)}, f32[1,256]{1,0:T(1,128)}, u32[]{:S(2)}) %copy-start.3) | copy-done | bytes 1048
  3.5 46.7 %shard_map.68 = (f32[1,384]{1,0:T(1,128)S(1)}, f32[32,384]{1,0:T(8,128)S(1)}) custom-call(f32[32,384]{1,0:T(8,128)S(1)} %copy-done, f32[32,256]{1,0:T(8,128)S(1)} %copy-done.1, f32[1,256]{1,0:T(1,128)S(1)} %copy-done.2, f32[1,256]{1,0:T(1,128)S(1)} %copy-done.3), custom_call_target="tpu_custom_call" | custom-call | tf_op jit(solution)/shard_map/pallas_call | solution.py:365
  50.2 0.0 copy-start.4
  50.3 0.7 %copy-done.4 = f32[384]{0:T(512)S(1)} copy-done((f32[384]{0:T(512)S(1)}, f32[384]{0:T(512)}, u32[]{:S(2)}) %copy-start.4) | copy-done | bytes 1560
  50.9 0.6 %multiply_add_fusion = f32[384]{0:T(512)} fusion(f32[384]{0:T(512)S(1)} %reduce, f32[384]{0:T(512)S(1)} %copy-done.4), kind=kLoop, calls=%fused_computation | loop fusion | flops 768 | bytes 4608 | tf_op jit(solution)/shard_map/add | solution.py:404
  51.5 0.6 %copy.8 = f32[32,384]{1,0:T(8,128)} copy(f32[32,384]{1,0:T(8,128)S(1)} %get-tuple-element.9) | data formatting | bytes 98304
  (1 shorter events, 0.0 us)
Async XLA Ops:
  0.6 0.8 %copy-start = (f32[32,384]{1,0:T(8,128)S(1)}, f32[32,384]{1,0:T(8,128)}, u32[]{:S(2)}) copy-start(f32[32,384]{1,0:T(8,128)} %x_hbm.1) | copy-start | bytes 147460
  1.4 0.8 %copy-start.1 = (f32[32,256]{1,0:T(8,128)S(1)}, f32[32,256]{1,0:T(8,128)}, u32[]{:S(2)}) copy-start(f32[32,256]{1,0:T(8,128)} %y_hbm.1) | copy-start | bytes 98308
  2.2 0.7 %copy-start.2 = (f32[1,256]{1,0:T(1,128)S(1)}, f32[1,256]{1,0:T(1,128)}, u32[]{:S(2)}) copy-start(f32[1,256]{1,0:T(1,128)} %g_hbm.1) | copy-start | bytes 3076
  2.9 0.7 %copy-start.3 = (f32[1,256]{1,0:T(1,128)S(1)}, f32[1,256]{1,0:T(1,128)}, u32[]{:S(2)}) copy-start(f32[1,256]{1,0:T(1,128)} %l_hbm.1) | copy-start | bytes 3076
  50.2 0.7 %copy-start.4 = (f32[384]{0:T(512)S(1)}, f32[384]{0:T(512)}, u32[]{:S(2)}) copy-start(f32[384]{0:T(512)} %param.6) | copy-start | bytes 4612

commit v2 on v1

v2 whole, which is shorter than its diff:
```python
import functools
import math

import jax
import jax.numpy as jnp
from jax import lax
from jax.experimental import pallas as pl
from jax.experimental.pallas import tpu as pltpu
from jax.sharding import PartitionSpec as P

ENTROPY = 4.0
LOG2E = math.log2(math.e)
LN2 = math.log(2.0)
MESH = pl.DeviceIdType.MESH
BF16, F32 = jnp.bfloat16, jnp.float32

NY, NZ, NX, CORES = 8, 8, 4, 2
DIMS, ROWS, COLS = 32, 384, 256
TILE = 256
GROUP = 4
SHARDS = NZ * CORES
BLOCKS = NY // CORES
SPAN = GROUP * COLS
TILES = BLOCKS * ROWS // TILE
DEPTH = 256
LANES = 128
COL_TALL = 72
PIECE_TALL = 40
OWNERS = ROWS // LANES

ORDER = (
    (0, 1, 2, 3, 4, 5, 6, 7),
    (1, 0, 2, 3, 4, 5, 6, 7),
    (2, 1, 3, 0, 4, 5, 6, 7),
    (3, 2, 4, 1, 0, 5, 6, 7),
    (4, 3, 5, 6, 7, 2, 1, 0),
    (5, 4, 6, 7, 3, 2, 1, 0),
    (6, 5, 7, 4, 3, 2, 1, 0),
    (7, 6, 5, 4, 3, 2, 1, 0),
)
TAKEN = (
    (-1, 0, 2, 3, 4, 5, 5),
    (-1, 0, 1, 2, 3, 3, 4),
    (-1, 0, 0, 1, 2, 2, 3),
    (-1, 0, 0, 0, 0, 1, 1),
    (-1, 0, 0, 0, 1, 1, 1),
    (-1, 0, 0, 1, 1, 1, 1),
    (-1, 0, 1, 1, 2, 2, 2),
    (-1, 1, 1, 2, 2, 2, 2),
)
NEAR_FIRST = (1, 7, 2, 6, 3, 5, 4)
EVEN = (4, 2, 6, 0)
ODD = (3, 5, 1, 7)


def split(value):
    first = value.astype(BF16)
    rest = value - first.astype(F32)
    second = rest.astype(BF16)
    third = (rest - second.astype(F32)).astype(BF16)
    return first, second, third


def kernel(
    x_hbm, y_hbm, g_hbm, l_hbm, pot_ref, bary_ref,
    xown, yown, gown, lown, xraw, craw, ya, yw, xa, s0, s1, m0, m1, mrun, acc, pout, pin, fin,
    in_sem, crecv, csend, fsend, rrecv, rsend, precv, psend, frecv, tsend, ready,
):
    src, tgt = lax.axis_index("src"), lax.axis_index("tgt")
    yi, zi = src // NZ, src % NZ
    xi, core = tgt // CORES, tgt % CORES
    odd = (yi + core) % 2
    home = odd == 0
    owner = jnp.logical_and(home, xi < OWNERS)

    def y_peer(e):
        return (((yi + e) % NY) * NZ + zi, tgt)

    def z_device(z):
        return (yi * NZ + z, tgt)

    def x_peer(e):
        return (src, ((xi + e) % NX) * CORES + core)

    def t_peer(e):
        return (src, (tgt + e) % (NX * CORES))

    sibling = (src, xi * CORES + 1 - core)

    def digits(table):
        packed = 0
        for z, row in enumerate(table):
            packed = packed + jnp.where(zi == z, sum(d * 8**i for i, d in enumerate(row)), 0)
        return [(packed // 8**i) % 8 for i in range(len(table[0]))]

    barrier = pltpu.get_barrier_semaphore()

    def greet(device):
        pl.semaphore_signal(barrier, inc=1, device_id=device, device_id_type=MESH)

    for z in range(NZ):

        @pl.when(jnp.logical_or(z > zi, z == zi - 1))
        def _(z=z):
            greet(z_device(z))

    for e in (4, 3, 5, 2, 6, 1, 7):
        if e % 2:
            greet(y_peer(e))
        else:

            @pl.when(home)
            def _(e=e):
                greet(y_peer(e))

    for e in range(1, NX):
        greet(x_peer(e))
    greet(sibling)

    loads = [
        pltpu.make_async_copy(a, b, in_sem.at[i])
        for i, (a, b) in enumerate(((x_hbm, xown), (y_hbm, yown), (g_hbm, gown), (l_hbm, lown)))
    ]
    for load in loads:
        load.start()
    mrun[...] = jnp.full_like(mrun, -1e30)
    acc[...] = jnp.zeros_like(acc)
    for load in loads:
        load.wait()

    y = yown[...]
    bias = (gown[...] - 0.5 * jnp.sum(y * y, axis=0, keepdims=True)) * (LOG2E / ENTROPY) + lown[...] * LOG2E
    for half in range(2):
        lanes = slice(half * LANES, (half + 1) * LANES)
        craw[zi, half * DIMS : (half + 1) * DIMS, :] = y[:, lanes]
    craw[zi, 64:72, :] = jnp.concatenate(
        [bias[:, :LANES], bias[:, LANES:], jnp.zeros((6, LANES), F32)], axis=0
    )

    order = digits(ORDER)
    taken = digits([[turn + 1 for turn in row] for row in TAKEN])
    pl.semaphore_wait(barrier, 7 - 3 * odd + zi + jnp.where(zi < NZ - 1, 1, 0) + NX)

    def column_copy(z):
        return pltpu.make_async_remote_copy(
            src_ref=craw.at[zi], dst_ref=craw.at[zi], send_sem=csend.at[z], recv_sem=crecv.at[zi],
            device_id=z_device(z), device_id_type=MESH,
        )

    def pass_copy(z):
        return pltpu.make_async_remote_copy(
            src_ref=craw.at[z], dst_ref=craw.at[NZ + z], send_sem=fsend.at[z], recv_sem=crecv.at[NZ + z],
            device_id=sibling, device_id_type=MESH,
        )

    def row_copy(e):
        back = (8 - e) % 8
        slot = EVEN.index(back) if back % 2 == 0 else ODD.index(back)
        return pltpu.make_async_remote_copy(
            src_ref=xown, dst_ref=xraw.at[slot], send_sem=rsend.at[e], recv_sem=rrecv.at[slot],
            device_id=y_peer(e), device_id_type=MESH,
        )

    pass_copy(zi).start()

    @pl.when(zi < NZ - 1)
    def _():
        column_copy(zi + 1).start()

    for e in range(1, NZ):

        @pl.when(zi >= e)
        def _(e=e):
            column_copy(zi - e).start()

    @pl.when(home)
    def _():
        for e in NEAR_FIRST:
            row_copy(e).start()

    def wait_column(place):
        pltpu.make_async_remote_copy(
            src_ref=craw.at[place], dst_ref=craw.at[place], send_sem=csend.at[0], recv_sem=crecv.at[place],
            device_id=sibling, device_id_type=MESH,
        ).wait_recv()

    def take(z):
        wait_column(z)
        pass_copy(z).start()

        @pl.when(z > zi + 1)
        def _():
            column_copy(z).start()

    def wait_rows(slot):
        pltpu.make_async_remote_copy(
            src_ref=xraw.at[slot], dst_ref=xraw.at[slot], send_sem=rsend.at[0], recv_sem=rrecv.at[slot],
            device_id=sibling, device_id_type=MESH,
        ).wait_recv()

    def prepare_rows(slot):
        x1, x2, x3 = split(xraw[slot] * (LOG2E / ENTROPY))
        row = lax.broadcasted_iota(jnp.int32, (64, ROWS), 0)
        ones = jnp.where(row < 3, 1.0, 0.0).astype(BF16)
        xa[:, slot * ROWS : (slot + 1) * ROWS] = jnp.concatenate([x1, x1, x2, x2, x1, x3, ones], axis=0)

    def prepare_columns(slot, place):
        raw = craw[slot]
        y1, y2, y3 = split(jnp.concatenate([raw[:32], raw[32:64]], axis=1))
        b = jnp.concatenate([raw[64:65], raw[65:66]], axis=1)
        b1 = b.astype(BF16).astype(F32)
        b2 = (b - b1).astype(BF16).astype(F32)
        b3 = b - b1 - b2
        row = lax.broadcasted_iota(jnp.int32, (64, COLS), 0)
        biases = jnp.where(row == 0, b1, jnp.where(row == 1, b2, jnp.where(row == 2, b3, 0.0))).astype(BF16)
        deep = jnp.concatenate([y1, y2, y1, y2, y3, y1, biases], axis=0)
        first = place * COLS if isinstance(place, int) else pl.multiple_of(place * COLS, COLS)
        ya[pl.ds(first, COLS), :] = deep.T
        yw[:, pl.ds(first, COLS)] = jnp.concatenate([y1, jnp.ones((16, COLS), BF16), y2], axis=0)

    def tile_lanes(tile):
        return pl.ds(pl.multiple_of(tile * TILE, TILE), TILE)

    def scores(group, tile, s, m):
        first = pl.multiple_of(group * SPAN, SPAN)
        value = jnp.dot(ya[pl.ds(first, SPAN), :], xa[:, tile_lanes(tile)], preferred_element_type=F32)
        s[...] = value
        m[...] = jnp.max(value.reshape(SPAN // 8, 8, TILE), axis=0)

    def absorb(group, tile, s, m):
        first = pl.multiple_of(group * SPAN, SPAN)
        lanes = tile_lanes(tile)
        old = mrun[0:1, lanes]
        new = jnp.maximum(old, jnp.max(m[...], axis=0, keepdims=True))
        mrun[0:1, lanes] = new
        share = jnp.exp2(s[...] - new)
        high = share.astype(BF16)
        low = (share - high.astype(F32)).astype(BF16)
        sums = jnp.dot(yw[:, pl.ds(first, SPAN)], high, preferred_element_type=F32)
        rest = jnp.dot(yw[0:48, pl.ds(first, SPAN)], low, preferred_element_type=F32)
        sums = jnp.concatenate([sums[:48] + rest, sums[48:]], axis=0)
        acc[:, lanes] = acc[:, lanes] * jnp.exp2(old - new) + sums

    def tile_at(step):
        group, place = step // TILES, step % TILES
        return group, jnp.where(group == 0, TILES - 1 - place, place)

    def block_offset(block):
        return EVEN[block] + odd * (ODD[block] - EVEN[block])

    def piece_copy(block, third):
        offset = block_offset(block)
        place = xi * NY + (NY - offset) % NY
        return pltpu.make_async_remote_copy(
            src_ref=pout.at[block * OWNERS + third], dst_ref=pin.at[place],
            send_sem=psend.at[block * OWNERS + third], recv_sem=precv.at[place],
            device_id=(((yi + offset) % NY) * NZ + zi, third * CORES + core), device_id_type=MESH,
        )

    def put_piece(ref, index, block, third):
        lanes = slice(block * ROWS + third * LANES, block * ROWS + (third + 1) * LANES)
        ref[index, 0:32, :] = acc[0:32, lanes] + acc[48:80, lanes]
        ref[index, 32:40, :] = jnp.concatenate(
            [acc[32:33, lanes], mrun[0:1, lanes], jnp.zeros((6, LANES), F32)], axis=0
        )

    def stays(block, third):
        return jnp.logical_and(block_offset(block) == 0, xi == third)

    def finish_block(block):
        for third in range(OWNERS):
            if block < 3:
                put_piece(pout, block * OWNERS + third, block, third)
                piece_copy(block, third).start()
            else:

                @pl.when(stays(block, third))
                def _(third=third):
                    put_piece(pin, xi * NY, block, third)

                @pl.when(jnp.logical_not(stays(block, third)))
                def _(third=third):
                    put_piece(pout, block * OWNERS + third, block, third)
                    piece_copy(block, third).start()

    @pl.when(home)
    def _():
        xraw[3] = xown[...]

    @pl.when(jnp.logical_not(home))
    def _():
        wait_rows(3)

    prepare_rows(3)
    first = order[1]
    take(first)
    wait_column(NZ + zi)
    prepare_columns(zi, 0)
    prepare_columns(NZ + zi, 1)
    prepare_columns(first, 2)
    wait_column(NZ + first)
    prepare_columns(NZ + first, 3)
    wait_rows(2)
    prepare_rows(2)
    scores(0, TILES - 1, s0, m0)

    last = SHARDS // GROUP * TILES - 1

    def two_steps(turn, carry):
        group, third = turn // 3, turn % 3

        @pl.when(turn == 1)
        def _():
            for slot in (1, 0):
                wait_rows(slot)
                prepare_rows(slot)
            for e in range(1, NX):
                pl.semaphore_signal(ready, inc=1, device_id=x_peer(e), device_id_type=MESH)

        for when in range(6):

            @pl.when(turn == when)
            def _(when=when):
                for i in range(1, NZ - 1):
                    if any(row[i] == when for row in TAKEN):

                        @pl.when(taken[i] == when + 1)
                        def _(i=i):
                            take(order[i + 1])

        step = turn * 2
        for half, (now, now_m, later, later_m) in enumerate(((s0, m0, s1, m1), (s1, m1, s0, m0))):
            g_now, t_now = tile_at(step + half)
            g_next, t_next = tile_at(jnp.minimum(step + half + 1, last))
            if half:
                for end in range(1, SHARDS // GROUP):

                    @pl.when(turn == 3 * end - 1)
                    def _(end=end):
                        for i in range(2):
                            z = order[2 * end + i]
                            prepare_columns(z, GROUP * end + 2 * i)
                            wait_column(NZ + z)
                            prepare_columns(NZ + z, GROUP * end + 2 * i + 1)

            scores(g_next, t_next, later, later_m)
            absorb(g_now, t_now, now, now_m)

        for when, block in ((9, 0), (10, 1)):

            @pl.when(turn == when)
            def _(block=block):
                if block == 0:
                    pl.semaphore_wait(ready, NX - 1)
                finish_block(block)

        return carry

    lax.fori_loop(0, 12, two_steps, 0)
    finish_block(2)
    finish_block(3)

    def result_copy(e):
        return pltpu.make_async_remote_copy(
            src_ref=fin.at[xi], dst_ref=fin.at[xi], send_sem=tsend.at[e], recv_sem=frecv.at[xi],
            device_id=t_peer(e), device_id_type=MESH,
        )

    @pl.when(owner)
    def _():
        for place in range(NX * NY):

            @pl.when(place != xi * NY)
            def _(place=place):
                pltpu.make_async_remote_copy(
                    src_ref=pin.at[place], dst_ref=pin.at[place], send_sem=psend.at[0], recv_sem=precv.at[place],
                    device_id=sibling, device_id_type=MESH,
                ).wait_recv()

        places = range(NX * NY)
        tops = [pin[place, 32:40, :] for place in places]
        peak = functools.reduce(jnp.maximum, tops)[1:2]
        factors = [jnp.exp2(top[1:2] - peak) for top in tops]
        total = functools.reduce(jnp.add, [top[0:1] * f for top, f in zip(tops, factors, strict=True)])
        weighted = functools.reduce(
            jnp.add, [pin[place, 0:32, :] * f for place, f in zip(places, factors, strict=True)]
        )
        fin[xi, 0:32, :] = weighted / total
        fin[xi, 32:40, :] = jnp.broadcast_to(peak * LN2 + jnp.log(total), (8, LANES))
        for e in range(1, NX * CORES):
            result_copy(e).start()

    x = xown[...]
    norm = 0.5 * jnp.sum(x * x, axis=0, keepdims=True)
    for third in range(OWNERS):

        @pl.when(jnp.logical_not(jnp.logical_and(home, xi == third)))
        def _(third=third):
            pltpu.make_async_remote_copy(
                src_ref=fin.at[third], dst_ref=fin.at[third], send_sem=tsend.at[0], recv_sem=frecv.at[third],
                device_id=sibling, device_id_type=MESH,
            ).wait_recv()

        lanes = slice(third * LANES, (third + 1) * LANES)
        bary_ref[:, lanes] = fin[third, 0:32, :]
        pot_ref[:, lanes] = norm[:, lanes] - ENTROPY * fin[third, 32:33, :]

    for z in range(NZ):

        @pl.when(zi != z)
        def _(z=z):
            column_copy(z).wait_send()

        pass_copy(z).wait_send()
    for block in range(BLOCKS):
        for third in range(OWNERS):
            if block < 3:
                piece_copy(block, third).wait_send()
            else:

                @pl.when(jnp.logical_not(stays(block, third)))
                def _(third=third):
                    piece_copy(block, third).wait_send()

    @pl.when(home)
    def _():
        for e in range(1, NY):
            row_copy(e).wait_send()

    @pl.when(owner)
    def _():
        for e in range(1, NX * CORES):
            result_copy(e).wait_send()


def on_device(src_points, src_logw, tgt_points, tgt_potential, tgt_logw):
    dma = pltpu.SemaphoreType.DMA
    vmem = pltpu.VMEM
    potential, barycentre = pl.pallas_call(
        kernel,
        out_shape=(jax.ShapeDtypeStruct((1, ROWS), F32), jax.ShapeDtypeStruct((DIMS, ROWS), F32)),
        in_specs=[pl.BlockSpec(memory_space=pl.ANY)] * 4,
        out_specs=(pl.BlockSpec(memory_space=pltpu.VMEM),) * 2,
        scratch_shapes=[
            vmem((DIMS, ROWS), F32),
            vmem((DIMS, COLS), F32),
            vmem((1, COLS), F32),
            vmem((1, COLS), F32),
            vmem((BLOCKS, DIMS, ROWS), F32),
            vmem((SHARDS, COL_TALL, LANES), F32),
            vmem((SHARDS * COLS, DEPTH), BF16),
            vmem((80, SHARDS * COLS), BF16),
            vmem((DEPTH, BLOCKS * ROWS), BF16),
            vmem((SPAN, TILE), F32),
            vmem((SPAN, TILE), F32),
            vmem((8, TILE), F32),
            vmem((8, TILE), F32),
            vmem((8, BLOCKS * ROWS), F32),
            vmem((80, BLOCKS * ROWS), F32),
            vmem((BLOCKS * OWNERS, PIECE_TALL, LANES), F32),
            vmem((NX * NY, PIECE_TALL, LANES), F32),
            vmem((OWNERS, PIECE_TALL, LANES), F32),
            dma((4,)),
            dma((SHARDS,)),
            dma((NZ,)),
            dma((NZ,)),
            dma((BLOCKS,)),
            dma((NY,)),
            dma((NX * NY,)),
            dma((BLOCKS * OWNERS,)),
            dma((OWNERS,)),
            dma((NX * CORES,)),
            pltpu.SemaphoreType.REGULAR,
        ],
        compiler_params=pltpu.CompilerParams(
            collective_id=0, has_side_effects=True, vmem_limit_bytes=63 * 2**20
        ),
    )(src_points, tgt_points, tgt_potential, tgt_logw)
    return ENTROPY * src_logw + potential[0], barycentre


def solution(mesh):
    return jax.shard_map(
        on_device,
        mesh=mesh,
        in_specs=(
            P(None, "src"),
            P("src"),
            P(None, ("tgt", "src")),
            P(None, ("tgt", "src")),
            P(None, ("tgt", "src")),
        ),
        out_specs=(P("src"), P(None, "src")),
        check_vma=False,
    )
```

time: 52.4 us -> 51 us (0.973)
  the two profiles are of different devices: /device:TPU:1 before, /device:TPU:385 now
where the time goes in v2:
time: 51 us; the launch traced here: 50.7 us
  Pallas kernels  46.7 us (92%)
  local copies, waits for them, and re-layouts  2.71 us (5%)
  between operations  0.65 us (1%)
  other arithmetic  0.6 us (1%)
    pallas_call x1, Pallas kernels, on_device(): pl.pallas_call(kernel, out_shape=(jax.ShapeDtypeStruct((1, ROWS), F32), j...  46.7 us
    unnamed x5, local copies, waits for them, and re-layouts  2.71 us

profile of v2, /device:TPU:385, one launch (start us, length us, event | category | flops | bytes accessed | tf_op | source)
XLA Modules:
  0.0 50.7 jit_solution(16467986890994396151)
XLA Ops:
  0.6 46.7 %shard_map.68 = (f32[1,384]{1,0:T(1,128)}, f32[32,384]{1,0:T(8,128)}) custom-call(f32[32,384]{1,0:T(8,128)} %x_hbm.1, f32[32,256]{1,0:T(8,128)} %y_hbm.1, f32[1,256]{1,0:T(1,128)} %g_hbm.1, f32[1,256]{1,0:T(1,128)} %l_hbm.1), custom_call_target="tpu_custom_call" | custom-call | tf_op jit(solution)/shard_map/pallas_call | solution.py:439
  47.4 0.0 copy-start.1
  47.4 0.6 %copy-done.1 = f32[1,384]{1,0:T(1,128)S(1)} copy-done((f32[1,384]{1,0:T(1,128)S(1)}, f32[1,384]{1,0:T(1,128)}, u32[]{:S(2)}) %copy-start.1) | copy-done | bytes 1560
  48.0 0.0 copy-start
  48.0 0.7 %copy-done = f32[384]{0:T(512)S(1)} copy-done((f32[384]{0:T(512)S(1)}, f32[384]{0:T(512)}, u32[]{:S(2)}) %copy-start) | copy-done | bytes 1560
  48.7 0.6 %multiply_add_fusion = f32[384]{0:T(512)} fusion(f32[384]{0:T(512)S(1)} %reduce, f32[384]{0:T(512)S(1)} %copy-done), kind=kLoop, calls=%fused_computation | loop fusion | flops 768 | bytes 4608 | tf_op jit(solution)/shard_map/add | solution.py:479
  49.3 1.4 %copy.8 = f32[32,384]{1,0:T(8,128)} copy(f32[32,384]{1,0:T(8,128)} %get-tuple-element.9) | data formatting | bytes 98304
  (1 shorter events, 0.0 us)
Async XLA Ops:
  47.4 0.6 %copy-start.1 = (f32[1,384]{1,0:T(1,128)S(1)}, f32[1,384]{1,0:T(1,128)}, u32[]{:S(2)}) copy-start(f32[1,384]{1,0:T(1,128)} %get-tuple-element.4) | copy-start | bytes 4612
  48.0 0.7 %copy-start = (f32[384]{0:T(512)S(1)}, f32[384]{0:T(512)}, u32[]{:S(2)}) copy-start(f32[384]{0:T(512)} %param.6) | copy-start | bytes 4612

commit v3 on v2

v3 whole, which is shorter than its diff:
```python
import functools
import math

import jax
import jax.numpy as jnp
from jax import lax
from jax.experimental import pallas as pl
from jax.experimental.pallas import tpu as pltpu
from jax.sharding import PartitionSpec as P

ENTROPY = 4.0
LOG2E = math.log2(math.e)
LN2 = math.log(2.0)
MESH = pl.DeviceIdType.MESH
BF16, F32 = jnp.bfloat16, jnp.float32

NY, NZ, NX, CORES = 8, 8, 4, 2
DIMS, ROWS, COLS = 32, 384, 256
TILE = 256
GROUP = 4
SHARDS = NZ * CORES
BLOCKS = NY // CORES
SPAN = GROUP * COLS
TILES = BLOCKS * ROWS // TILE
REST = SHARDS * COLS - 2 * SPAN
DEPTH = 256
LANES = 128
COL_TALL = 72
PIECE_TALL = 40
OWNERS = ROWS // LANES

DIRECT = {0: 0, 1: 2, 7: 3, 2: 6, 6: 7, 3: 10, 5: 11, 4: 14}
PASSED = {0: 1, 1: 4, 7: 5, 2: 8, 6: 9, 3: 12, 5: 13, 4: 15}
NEAR_FIRST = (1, 7, 2, 6, 3, 5, 4)

EVEN = (4, 2, 6, 0)
ODD = (3, 5, 1, 7)


def split(value):
    first = value.astype(BF16)
    rest = value - first.astype(F32)
    second = rest.astype(BF16)
    third = (rest - second.astype(F32)).astype(BF16)
    return first, second, third


def kernel(
    x_hbm, w_hbm, y_hbm, g_hbm, l_hbm, pot_ref, bary_ref,
    xown, wown, yown, gown, lown, xraw, craw, ya, yw, xa, s0, s1, m0, m1, mrun, acc, pout, pin, fin,
    in_sem, crecv, csend, fsend, rrecv, rsend, precv, psend, frecv, tsend, ready, ready_two,
):
    src, tgt = lax.axis_index("src"), lax.axis_index("tgt")
    yi, zi = src // NZ, src % NZ
    xi, core = tgt // CORES, tgt % CORES
    odd = (yi + core) % 2
    home = odd == 0
    owner = jnp.logical_and(core == 1, xi < OWNERS)

    def y_peer(e):
        return (((yi + e) % NY) * NZ + zi, tgt)

    def z_peer(e):
        return (yi * NZ + (zi + e) % NZ, tgt)

    def x_peer(e):
        return (src, ((xi + e) % NX) * CORES + core)

    def t_peer(e):
        return (src, (tgt + e) % (NX * CORES))

    sibling = (src, xi * CORES + 1 - core)

    barrier = pltpu.get_barrier_semaphore()

    def greet(device):
        pl.semaphore_signal(barrier, inc=1, device_id=device, device_id_type=MESH)

    for e in reversed(NEAR_FIRST):
        greet(z_peer(e))
        if e % 2:
            greet(y_peer(e))
        else:

            @pl.when(home)
            def _(e=e):
                greet(y_peer(e))

    for e in (1, NX - 1):
        greet(x_peer(e))
    greet(sibling)

    loads = [
        pltpu.make_async_copy(a, b, in_sem.at[i])
        for i, (a, b) in enumerate(((x_hbm, xown), (y_hbm, yown), (g_hbm, gown), (l_hbm, lown), (w_hbm, wown)))
    ]
    for load in loads:
        load.start()
    mrun[...] = jnp.full_like(mrun, -1e30)
    acc[...] = jnp.zeros_like(acc)
    for load in loads:
        load.wait()

    y = yown[...]
    bias = (gown[...] - 0.5 * jnp.sum(y * y, axis=0, keepdims=True)) * (LOG2E / ENTROPY) + lown[...] * LOG2E
    for half in range(2):
        lanes = slice(half * LANES, (half + 1) * LANES)
        craw[0, half * DIMS : (half + 1) * DIMS, :] = y[:, lanes]
    craw[0, 64:72, :] = jnp.concatenate(
        [bias[:, :LANES], bias[:, LANES:], jnp.zeros((6, LANES), F32)], axis=0
    )

    @pl.when(home)
    def _():
        xraw[3] = xown[...]

    pl.semaphore_wait(barrier, 17 - 3 * odd)

    def column_copy(e):
        place = DIRECT[(8 - e) % 8]
        return pltpu.make_async_remote_copy(
            src_ref=craw.at[0], dst_ref=craw.at[place], send_sem=csend.at[0], recv_sem=crecv.at[place],
            device_id=z_peer(e), device_id_type=MESH,
        )

    def pass_copy(e):
        return pltpu.make_async_remote_copy(
            src_ref=craw.at[DIRECT[e]], dst_ref=craw.at[PASSED[e]], send_sem=fsend.at[0],
            recv_sem=crecv.at[PASSED[e]], device_id=sibling, device_id_type=MESH,
        )

    def row_copy(e):
        back = (8 - e) % 8
        slot = EVEN.index(back) if back % 2 == 0 else ODD.index(back)
        return pltpu.make_async_remote_copy(
            src_ref=xown, dst_ref=xraw.at[slot], send_sem=rsend.at[e], recv_sem=rrecv.at[slot],
            device_id=y_peer(e), device_id_type=MESH,
        )

    pass_copy(0).start()
    for e in NEAR_FIRST:
        column_copy(e).start()

        @pl.when(home)
        def _(e=e):
            row_copy(e).start()

    def wait_column(place):
        pltpu.make_async_remote_copy(
            src_ref=craw.at[place], dst_ref=craw.at[place], send_sem=csend.at[0], recv_sem=crecv.at[place],
            device_id=sibling, device_id_type=MESH,
        ).wait_recv()

    def take(*places):
        for e in places:
            wait_column(DIRECT[e])
            pass_copy(e).start()

    def wait_rows(slot):
        pltpu.make_async_remote_copy(
            src_ref=xraw.at[slot], dst_ref=xraw.at[slot], send_sem=rsend.at[0], recv_sem=rrecv.at[slot],
            device_id=sibling, device_id_type=MESH,
        ).wait_recv()

    def prepare_rows(slot):
        x1, x2, x3 = split(xraw[slot] * (LOG2E / ENTROPY))
        row = lax.broadcasted_iota(jnp.int32, (64, ROWS), 0)
        ones = jnp.where(row < 3, 1.0, 0.0).astype(BF16)
        xa[:, slot * ROWS : (slot + 1) * ROWS] = jnp.concatenate([x1, x1, x2, x2, x1, x3, ones], axis=0)

    def prepare_columns(place):
        raw = craw[place]
        y1, y2, y3 = split(jnp.concatenate([raw[:32], raw[32:64]], axis=1))
        b = jnp.concatenate([raw[64:65], raw[65:66]], axis=1)
        b1 = b.astype(BF16).astype(F32)
        b2 = (b - b1).astype(BF16).astype(F32)
        b3 = b - b1 - b2
        row = lax.broadcasted_iota(jnp.int32, (64, COLS), 0)
        biases = jnp.where(row == 0, b1, jnp.where(row == 1, b2, jnp.where(row == 2, b3, 0.0))).astype(BF16)
        deep = jnp.concatenate([y1, y2, y1, y2, y3, y1, biases], axis=0)
        first = place * COLS
        ya[pl.ds(first, COLS), :] = deep.T
        yw[:, pl.ds(first, COLS)] = jnp.concatenate([y1, jnp.ones((16, COLS), BF16), y2], axis=0)

    def tile_lanes(tile):
        return pl.ds(pl.multiple_of(tile * TILE, TILE), TILE)

    def scores(first, span, tile, s, m):
        value = jnp.dot(ya[pl.ds(first, span), :], xa[:, tile_lanes(tile)], preferred_element_type=F32)
        s[0:span, :] = value
        m[...] = jnp.max(value.reshape(span // 8, 8, TILE), axis=0)

    def absorb(first, span, tile, s, m):
        lanes = tile_lanes(tile)
        old = mrun[0:1, lanes]
        new = jnp.maximum(old, jnp.max(m[...], axis=0, keepdims=True))
        mrun[0:1, lanes] = new
        share = jnp.exp2(s[0:span, :] - new)
        high = share.astype(BF16)
        low = (share - high.astype(F32)).astype(BF16)
        sums = jnp.dot(yw[:, pl.ds(first, span)], high, preferred_element_type=F32)
        rest = jnp.dot(yw[0:48, pl.ds(first, span)], low, preferred_element_type=F32)
        sums = jnp.concatenate([sums[:48] + rest, sums[48:]], axis=0)
        acc[:, lanes] = acc[:, lanes] * jnp.exp2(old - new) + sums

    def block_offset(block):
        return EVEN[block] + odd * (ODD[block] - EVEN[block])

    def piece_copy(block, third):
        offset = block_offset(block)
        place = xi * NY + (NY - offset) % NY
        return pltpu.make_async_remote_copy(
            src_ref=pout.at[block * OWNERS + third], dst_ref=pin.at[place],
            send_sem=psend.at[0], recv_sem=precv.at[0],
            device_id=(((yi + offset) % NY) * NZ + zi, third * CORES + 1), device_id_type=MESH,
        )

    def put_piece(ref, index, block, third):
        lanes = slice(block * ROWS + third * LANES, block * ROWS + (third + 1) * LANES)
        ref[index, 0:32, :] = acc[0:32, lanes] + acc[48:80, lanes]
        ref[index, 32:40, :] = jnp.concatenate(
            [acc[32:33, lanes], mrun[0:1, lanes], jnp.zeros((6, LANES), F32)], axis=0
        )

    def stays(block, third):
        return jnp.logical_and(jnp.logical_and(home, core == 1), xi == third)

    def finish_block(block):
        for third in range(OWNERS):
            if block < 3:
                put_piece(pout, block * OWNERS + third, block, third)
                piece_copy(block, third).start()
            else:

                put_piece(pout, block * OWNERS + third, block, third)

                @pl.when(stays(block, third))
                def _(third=third):
                    pltpu.make_async_copy(
                        pout.at[block * OWNERS + third], pin.at[xi * NY], precv.at[0]
                    ).start()

                @pl.when(jnp.logical_not(stays(block, third)))
                def _(third=third):
                    piece_copy(block, third).start()

    def prepare_group(group):
        for place in range(group * GROUP, (group + 1) * GROUP):
            if place > 0 and place not in (2, 3, 6, 7, 10, 11, 14):
                wait_column(place)
            prepare_columns(place)

    def take_rows(slot):
        wait_rows(slot)
        prepare_rows(slot)

    @pl.when(home)
    def _():
        prepare_rows(3)

    @pl.when(jnp.logical_not(home))
    def _():
        take_rows(3)

    take(1, 7)
    prepare_group(0)

    scores(0, SPAN, 5, s0, m0)
    take_rows(2)
    scores(0, SPAN, 4, s1, m1)
    absorb(0, SPAN, 5, s0, m0)
    take(2, 6)
    scores(0, SPAN, 3, s0, m0)
    absorb(0, SPAN, 4, s1, m1)
    take_rows(1)
    scores(0, SPAN, 2, s1, m1)
    absorb(0, SPAN, 3, s0, m0)
    take_rows(0)
    for e in (1, NX - 1):
        pl.semaphore_signal(ready, inc=1, device_id=x_peer(e), device_id_type=MESH)
    scores(0, SPAN, 1, s0, m0)
    absorb(0, SPAN, 2, s1, m1)
    take(3, 5)
    scores(0, SPAN, 0, s1, m1)
    absorb(0, SPAN, 1, s0, m0)
    prepare_group(1)

    scores(SPAN, SPAN, 0, s0, m0)
    absorb(0, SPAN, 0, s1, m1)
    take(4)
    for tile in range(0, TILES - 2, 2):
        scores(SPAN, SPAN, tile + 1, s1, m1)
        absorb(SPAN, SPAN, tile, s0, m0)
        scores(SPAN, SPAN, tile + 2, s0, m0)
        absorb(SPAN, SPAN, tile + 1, s1, m1)
    scores(SPAN, SPAN, TILES - 1, s1, m1)
    absorb(SPAN, SPAN, TILES - 2, s0, m0)
    for group in range(2, SHARDS // GROUP):
        prepare_group(group)
    pl.semaphore_wait(ready, 2)
    for e in (1, NX - 1):
        pl.semaphore_signal(ready_two, inc=1, device_id=x_peer(e), device_id_type=MESH)

    rest = 2 * SPAN
    scores(rest, REST, 0, s0, m0)
    absorb(SPAN, SPAN, TILES - 1, s1, m1)

    def two_tiles(turn, carry):
        scores(rest, REST, 2 * turn + 1, s1, m1)
        absorb(rest, REST, 2 * turn, s0, m0)

        @pl.when(turn == 1)
        def _():
            finish_block(1)

        scores(rest, REST, 2 * turn + 2, s0, m0)
        absorb(rest, REST, 2 * turn + 1, s1, m1)

        @pl.when(turn == 0)
        def _():
            pl.semaphore_wait(ready_two, 2)
            finish_block(0)

        return carry

    lax.fori_loop(0, 2, two_tiles, 0)
    scores(rest, REST, TILES - 1, s1, m1)
    absorb(rest, REST, TILES - 2, s0, m0)
    finish_block(2)
    absorb(rest, REST, TILES - 1, s1, m1)
    finish_block(3)

    def result_copy(e):
        return pltpu.make_async_remote_copy(
            src_ref=fin.at[xi], dst_ref=fin.at[xi], send_sem=tsend.at[0], recv_sem=frecv.at[xi],
            device_id=t_peer(e), device_id_type=MESH,
        )

    @pl.when(owner)
    def _():
        pltpu.make_async_copy(pin, pin, precv.at[0]).wait()
        places = range(NX * NY)
        tops = [pin[place, 32:40, :] for place in places]
        peak = functools.reduce(jnp.maximum, tops)[1:2]
        factors = [jnp.exp2(top[1:2] - peak) for top in tops]
        total = functools.reduce(jnp.add, [top[0:1] * f for top, f in zip(tops, factors, strict=True)])
        weighted = functools.reduce(
            jnp.add, [pin[place, 0:32, :] * f for place, f in zip(places, factors, strict=True)]
        )
        fin[xi, 0:32, :] = weighted / total
        fin[xi, 32:40, :] = jnp.broadcast_to(peak * LN2 + jnp.log(total), (8, LANES))
        for e in (4, 3, 5, 2, 6, 1, 7):
            result_copy(e).start()

    x = xown[...]
    norm = 0.5 * jnp.sum(x * x, axis=0, keepdims=True)
    for third in range(OWNERS):

        @pl.when(jnp.logical_not(jnp.logical_and(core == 1, xi == third)))
        def _(third=third):
            pltpu.make_async_remote_copy(
                src_ref=fin.at[third], dst_ref=fin.at[third], send_sem=tsend.at[0], recv_sem=frecv.at[third],
                device_id=sibling, device_id_type=MESH,
            ).wait_recv()

        lanes = slice(third * LANES, (third + 1) * LANES)
        bary_ref[:, lanes] = fin[third, 0:32, :]
        pot_ref[lanes] = ENTROPY * wown[lanes] + (norm[:, lanes] - ENTROPY * fin[third, 32:33, :]).reshape(LANES)

    def wait_sent(ref, sem):
        pltpu.make_async_remote_copy(
            src_ref=ref, dst_ref=ref, send_sem=sem, recv_sem=crecv.at[0], device_id=sibling, device_id_type=MESH
        ).wait_send()

    wait_sent(craw.at[pl.ds(0, NZ - 1)], csend.at[0])
    wait_sent(craw.at[pl.ds(0, NZ)], fsend.at[0])
    keeps = jnp.logical_and(home, owner)

    @pl.when(keeps)
    def _():
        wait_sent(pout.at[pl.ds(0, BLOCKS * OWNERS - 1)], psend.at[0])

    @pl.when(jnp.logical_not(keeps))
    def _():
        wait_sent(pout, psend.at[0])

    @pl.when(home)
    def _():
        for e in range(1, NY):
            row_copy(e).wait_send()

    @pl.when(owner)
    def _():
        wait_sent(pin.at[pl.ds(0, NX * CORES - 1)], tsend.at[0])


def hand_over(pot_in, bary_in, pot_out, bary_out):
    pot_out[...] = pot_in[...]
    bary_out[...] = bary_in[...]


def on_device(src_points, src_logw, tgt_points, tgt_potential, tgt_logw):
    dma = pltpu.SemaphoreType.DMA
    vmem = pltpu.VMEM
    shapes = (jax.ShapeDtypeStruct((ROWS,), F32), jax.ShapeDtypeStruct((DIMS, ROWS), F32))
    results = pl.pallas_call(
        kernel,
        out_shape=shapes,
        in_specs=[pl.BlockSpec(memory_space=pl.ANY)] * 5,
        out_specs=(pl.BlockSpec(memory_space=vmem),) * 2,
        scratch_shapes=[
            vmem((DIMS, ROWS), F32),
            vmem((ROWS,), F32),
            vmem((DIMS, COLS), F32),
            vmem((1, COLS), F32),
            vmem((1, COLS), F32),
            vmem((BLOCKS, DIMS, ROWS), F32),
            vmem((SHARDS, COL_TALL, LANES), F32),
            vmem((SHARDS * COLS, DEPTH), BF16),
            vmem((80, SHARDS * COLS), BF16),
            vmem((DEPTH, BLOCKS * ROWS), BF16),
            vmem((REST, TILE), F32),
            vmem((REST, TILE), F32),
            vmem((8, TILE), F32),
            vmem((8, TILE), F32),
            vmem((8, BLOCKS * ROWS), F32),
            vmem((80, BLOCKS * ROWS), F32),
            vmem((BLOCKS * OWNERS, PIECE_TALL, LANES), F32),
            vmem((NX * NY, PIECE_TALL, LANES), F32),
            vmem((OWNERS, PIECE_TALL, LANES), F32),
            dma((5,)),
            dma((SHARDS,)),
            dma((1,)),
            dma((1,)),
            dma((BLOCKS,)),
            dma((NY,)),
            dma((1,)),
            dma((1,)),
            dma((OWNERS,)),
            dma((1,)),
            pltpu.SemaphoreType.REGULAR,
            pltpu.SemaphoreType.REGULAR,
        ],
        compiler_params=pltpu.CompilerParams(
            collective_id=0, has_side_effects=True, vmem_limit_bytes=63 * 2**20
        ),
    )(src_points, src_logw, tgt_points, tgt_potential, tgt_logw)
    return pl.pallas_call(
        hand_over,
        out_shape=shapes,
        in_specs=[pl.BlockSpec(memory_space=vmem)] * 2,
        out_specs=(pl.BlockSpec(memory_space=vmem),) * 2,
    )(*results)


def solution(mesh):
    return jax.shard_map(
        on_device,
        mesh=mesh,
        in_specs=(
            P(None, "src"),
            P("src"),
            P(None, ("tgt", "src")),
            P(None, ("tgt", "src")),
            P(None, ("tgt", "src")),
        ),
        out_specs=(P("src"), P(None, "src")),
        check_vma=False,
    )
```

time: 51 us -> 44.4 us (0.87)
  the two profiles are of different devices: /device:TPU:385 before, /device:TPU:1 now
where the time goes in v3:
time: 44.4 us; the launch traced here: 44.2 us
  Pallas kernels  43.6 us (98%)
  between operations  0.64 us (1%)
    pallas_call x1, Pallas kernels, on_device(): pl.pallas_call(kernel, out_shape=shapes, in_specs=[pl.BlockSpec(memory_sp...  42.1 us
    pallas_call x1, Pallas kernels, on_device(): pl.pallas_call(hand_over, out_shape=shapes, in_specs=[pl.BlockSpec(memory...  1.43 us

profile of v3, /device:TPU:1, one launch (start us, length us, event | category | flops | bytes accessed | tf_op | source)
XLA Modules:
  0.0 44.2 jit_solution(7227573463755677811)
XLA Ops:
  0.6 42.1 %shard_map.68 = (f32[384]{0:T(512)}, f32[32,384]{1,0:T(8,128)}) custom-call(f32[32,384]{1,0:T(8,128)} %x_hbm.1, f32[384]{0:T(512)} %w_hbm.1, f32[32,256]{1,0:T(8,128)} %y_hbm.1, f32[1,256]{1,0:T(1,128)} %g_hbm.1, f32[1,256]{1,0:T(1,128)} %l_hbm.1), custom_call_target="tpu_custom_call" | custom-call | tf_op jit(solution)/shard_map/pallas_call | solution.py:406
  42.8 1.4 %shard_map.69 = (f32[384]{0:T(512)}, f32[32,384]{1,0:T(8,128)}) custom-call(f32[384]{0:T(512)} %get-tuple-element.4.pot_in, f32[32,384]{1,0:T(8,128)} %get-tuple-element.5.bary_in), custom_call_target="tpu_custom_call" | custom-call | tf_op jit(solution)/shard_map/pallas_call | solution.py:448

commit v4 on v3

--- a/solution.py
+++ b/solution.py
@@ -29,9 +29,12 @@
 PIECE_TALL = 40
 OWNERS = ROWS // LANES
 
-DIRECT = {0: 0, 1: 2, 7: 3, 2: 6, 6: 7, 3: 10, 5: 11, 4: 14}
-PASSED = {0: 1, 1: 4, 7: 5, 2: 8, 6: 9, 3: 12, 5: 13, 4: 15}
-NEAR_FIRST = (1, 7, 2, 6, 3, 5, 4)
+COLUMNS = (0, 8, 1, 2, 9, 10, 3, 11, 4, 12, 5, 13, 6, 14, 7, 15)
+SPOT = {place: spot for spot, place in enumerate(COLUMNS)}
+LOW = 4
+
+NEAR = (1, 7)
+FAR = (2, 6, 3, 5)
 
 EVEN = (4, 2, 6, 0)
 ODD = (3, 5, 1, 7)
@@ -48,20 +51,23 @@
 def kernel(
     x_hbm, w_hbm, y_hbm, g_hbm, l_hbm, pot_ref, bary_ref,
     xown, wown, yown, gown, lown, xraw, craw, ya, yw, xa, s0, s1, m0, m1, mrun, acc, pout, pin, fin,
-    in_sem, crecv, csend, fsend, rrecv, rsend, precv, psend, frecv, tsend, ready, ready_two,
+    in_sem, crecv, csend, fsend, rrecv, rsend, precv, psend, frecv, tsend, ready, ready_two, later_in,
 ):
     src, tgt = lax.axis_index("src"), lax.axis_index("tgt")
     yi, zi = src // NZ, src % NZ
     xi, core = tgt // CORES, tgt % CORES
     odd = (yi + core) % 2
     home = odd == 0
+    low = zi < LOW
     owner = jnp.logical_and(core == 1, xi < OWNERS)
 
     def y_peer(e):
         return (((yi + e) % NY) * NZ + zi, tgt)
 
-    def z_peer(e):
-        return (yi * NZ + (zi + e) % NZ, tgt)
+    def z_peer(tie):
+        bits = [(zi // 2**i) % 2 for i in range(3)]
+        z = sum((1 - bit if tie // 2**i % 2 else bit) * 2**i for i, bit in enumerate(bits))
+        return (yi * NZ + z, tgt)
 
     def x_peer(e):
         return (src, ((xi + e) % NX) * CORES + core)
@@ -76,8 +82,14 @@
     def greet(device):
         pl.semaphore_signal(barrier, inc=1, device_id=device, device_id_type=MESH)
 
-    for e in reversed(NEAR_FIRST):
-        greet(z_peer(e))
+    @pl.when(low)
+    def _():
+        for tie in range(LOW, NZ):
+            greet(z_peer(tie))
+
+    for tie in (3, 2, 1):
+        greet(z_peer(tie))
+    for e in reversed(NEAR + FAR):
         if e % 2:
             greet(y_peer(e))
         else:
@@ -114,19 +126,18 @@
     def _():
         xraw[3] = xown[...]
 
-    pl.semaphore_wait(barrier, 17 - 3 * odd)
-
-    def column_copy(e):
-        place = DIRECT[(8 - e) % 8]
+    pl.semaphore_wait(barrier, 16 - 2 * odd - 4 * jnp.where(low, 1, 0))
+
+    def column_copy(tie):
         return pltpu.make_async_remote_copy(
-            src_ref=craw.at[0], dst_ref=craw.at[place], send_sem=csend.at[0], recv_sem=crecv.at[place],
-            device_id=z_peer(e), device_id_type=MESH,
-        )
-
-    def pass_copy(e):
+            src_ref=craw.at[0], dst_ref=craw.at[tie], send_sem=csend.at[0], recv_sem=crecv.at[tie],
+            device_id=z_peer(tie), device_id_type=MESH,
+        )
+
+    def pass_copy(tie):
         return pltpu.make_async_remote_copy(
-            src_ref=craw.at[DIRECT[e]], dst_ref=craw.at[PASSED[e]], send_sem=fsend.at[0],
-            recv_sem=crecv.at[PASSED[e]], device_id=sibling, device_id_type=MESH,
+            src_ref=craw.at[tie], dst_ref=craw.at[NZ + tie], send_sem=fsend.at[0],
+            recv_sem=crecv.at[NZ + tie], device_id=sibling, device_id_type=MESH,
         )
 
     def row_copy(e):
@@ -137,13 +148,21 @@
             device_id=y_peer(e), device_id_type=MESH,
         )
 
-    pass_copy(0).start()
-    for e in NEAR_FIRST:
-        column_copy(e).start()
-
+    def last_row_copy():
+        return pltpu.make_async_remote_copy(
+            src_ref=xraw.at[0], dst_ref=xraw.at[0], send_sem=rsend.at[4], recv_sem=rrecv.at[0],
+            device_id=y_peer(7), device_id_type=MESH,
+        )
+
+    def send_rows(places):
         @pl.when(home)
-        def _(e=e):
-            row_copy(e).start()
+        def _():
+            for e in places:
+                row_copy(e).start()
+
+    def across():
+        for tie in range(LOW, NZ):
+            column_copy(tie).start()
 
     def wait_column(place):
         pltpu.make_async_remote_copy(
@@ -151,10 +170,10 @@
             device_id=sibling, device_id_type=MESH,
         ).wait_recv()
 
-    def take(*places):
-        for e in places:
-            wait_column(DIRECT[e])
-            pass_copy(e).start()
+    def take(*ties):
+        for tie in ties:
+            wait_column(tie)
+            pass_copy(tie).start()
 
     def wait_rows(slot):
         pltpu.make_async_remote_copy(
@@ -178,7 +197,7 @@
         row = lax.broadcasted_iota(jnp.int32, (64, COLS), 0)
         biases = jnp.where(row == 0, b1, jnp.where(row == 1, b2, jnp.where(row == 2, b3, 0.0))).astype(BF16)
         deep = jnp.concatenate([y1, y2, y1, y2, y3, y1, biases], axis=0)
-        first = place * COLS
+        first = SPOT[place] * COLS
         ya[pl.ds(first, COLS), :] = deep.T
         yw[:, pl.ds(first, COLS)] = jnp.concatenate([y1, jnp.ones((16, COLS), BF16), y2], axis=0)
 
@@ -225,110 +244,146 @@
     def stays(block, third):
         return jnp.logical_and(jnp.logical_and(home, core == 1), xi == third)
 
-    def finish_block(block):
-        for third in range(OWNERS):
+    def finish_tile(tile):
+        for unit in range(tile * TILE // LANES, (tile + 1) * TILE // LANES):
+            block, third = unit // OWNERS, unit % OWNERS
+            put_piece(pout, unit, block, third)
             if block < 3:
-                put_piece(pout, block * OWNERS + third, block, third)
                 piece_copy(block, third).start()
             else:
 
-                put_piece(pout, block * OWNERS + third, block, third)
-
                 @pl.when(stays(block, third))
-                def _(third=third):
-                    pltpu.make_async_copy(
-                        pout.at[block * OWNERS + third], pin.at[xi * NY], precv.at[0]
-                    ).start()
+                def _(unit=unit):
+                    pltpu.make_async_copy(pout.at[unit], pin.at[xi * NY], precv.at[0]).start()
 
                 @pl.when(jnp.logical_not(stays(block, third)))
-                def _(third=third):
+                def _(block=block, third=third):
                     piece_copy(block, third).start()
 
-    def prepare_group(group):
-        for place in range(group * GROUP, (group + 1) * GROUP):
-            if place > 0 and place not in (2, 3, 6, 7, 10, 11, 14):
-                wait_column(place)
+    def prepare(*places):
+        for place in places:
             prepare_columns(place)
+
+    def arrived(*ties):
+        for tie in ties:
+            wait_column(NZ + tie)
 
     def take_rows(slot):
         wait_rows(slot)
         prepare_rows(slot)
 
+    pass_copy(0).start()
+    column_copy(1).start()
+    send_rows(NEAR)
+
+    @pl.when(jnp.logical_not(low))
+    def _():
+        across()
+        for tie in range(LOW, NZ):
+            pl.semaphore_signal(later_in, inc=1, device_id=z_peer(tie), device_id_type=MESH)
+
+    column_copy(2).start()
+    prepare(0)
+
     @pl.when(home)
     def _():
         prepare_rows(3)
 
+    column_copy(3).start()
+    send_rows(FAR)
+
     @pl.when(jnp.logical_not(home))
     def _():
         take_rows(3)
 
-    take(1, 7)
-    prepare_group(0)
-
-    scores(0, SPAN, 5, s0, m0)
+    arrived(0)
+    take(1, 2)
+    prepare(8, 1, 2)
+
+    buffers = ((s0, m0), (s1, m1))
+
+    def step(number, done, following):
+        if following is not None:
+            scores(*following, *buffers[(number + 1) % 2])
+        if done is not None:
+            absorb(*done, *buffers[number % 2])
+
+    one, two, rest = (0, SPAN), (SPAN, SPAN), (2 * SPAN, REST)
+
+    step(-1, None, (*one, 5))
     take_rows(2)
-    scores(0, SPAN, 4, s1, m1)
-    absorb(0, SPAN, 5, s0, m0)
-    take(2, 6)
-    scores(0, SPAN, 3, s0, m0)
-    absorb(0, SPAN, 4, s1, m1)
+    step(0, (*one, 5), (*one, 4))
+    take(3)
+    step(1, (*one, 4), (*one, 3))
     take_rows(1)
-    scores(0, SPAN, 2, s1, m1)
-    absorb(0, SPAN, 3, s0, m0)
-    take_rows(0)
+
+    @pl.when(jnp.logical_not(home))
+    def _():
+        wait_rows(0)
+        last_row_copy().start()
+        prepare_rows(0)
+
+    step(2, (*one, 3), (*one, 2))
+    arrived(1, 2, 3)
+    prepare(9, 10, 3, 11)
+    step(3, (*one, 2), (*two, 5))
+
+    @pl.when(low)
+    def _():
+        pl.semaphore_wait(later_in, NZ - LOW)
+        across()
+
+    step(4, (*two, 5), (*two, 4))
+    step(5, (*two, 4), (*two, 3))
+    step(6, (*two, 3), (*two, 2))
+
+    @pl.when(home)
+    def _():
+        take_rows(0)
+
     for e in (1, NX - 1):
         pl.semaphore_signal(ready, inc=1, device_id=x_peer(e), device_id_type=MESH)
-    scores(0, SPAN, 1, s0, m0)
-    absorb(0, SPAN, 2, s1, m1)
-    take(3, 5)
-    scores(0, SPAN, 0, s1, m1)
-    absorb(0, SPAN, 1, s0, m0)
-    prepare_group(1)
-
-    scores(SPAN, SPAN, 0, s0, m0)
-    absorb(0, SPAN, 0, s1, m1)
-    take(4)
-    for tile in range(0, TILES - 2, 2):
-        scores(SPAN, SPAN, tile + 1, s1, m1)
-        absorb(SPAN, SPAN, tile, s0, m0)
-        scores(SPAN, SPAN, tile + 2, s0, m0)
-        absorb(SPAN, SPAN, tile + 1, s1, m1)
-    scores(SPAN, SPAN, TILES - 1, s1, m1)
-    absorb(SPAN, SPAN, TILES - 2, s0, m0)
-    for group in range(2, SHARDS // GROUP):
-        prepare_group(group)
+    step(7, (*two, 2), (*one, 1))
+    step(8, (*one, 1), (*one, 0))
+    take(7, 6, 5, 4)
+    prepare(7, 6, 5, 4)
+    step(9, (*one, 0), (*two, 1))
     pl.semaphore_wait(ready, 2)
     for e in (1, NX - 1):
         pl.semaphore_signal(ready_two, inc=1, device_id=x_peer(e), device_id_type=MESH)
-
-    rest = 2 * SPAN
-    scores(rest, REST, 0, s0, m0)
-    absorb(SPAN, SPAN, TILES - 1, s1, m1)
+    step(10, (*two, 1), (*two, 0))
+    arrived(7, 6, 5, 4)
+    prepare(15, 14, 13, 12)
+
+    step(11, (*two, 0), (*rest, 0))
 
     def two_tiles(turn, carry):
-        scores(rest, REST, 2 * turn + 1, s1, m1)
-        absorb(rest, REST, 2 * turn, s0, m0)
-
-        @pl.when(turn == 1)
-        def _():
-            finish_block(1)
-
-        scores(rest, REST, 2 * turn + 2, s0, m0)
-        absorb(rest, REST, 2 * turn + 1, s1, m1)
-
-        @pl.when(turn == 0)
-        def _():
-            pl.semaphore_wait(ready_two, 2)
-            finish_block(0)
+        scores(*rest, 2 * turn + 1, s1, m1)
+        absorb(*rest, 2 * turn, s0, m0)
+        for when in range(2):
+
+            @pl.when(turn == when)
+            def _(when=when):
+                if when == 0:
+                    pl.semaphore_wait(ready_two, 2)
+                finish_tile(2 * when)
+
+        scores(*rest, 2 * turn + 2, s0, m0)
+        absorb(*rest, 2 * turn + 1, s1, m1)
+        for when in range(2):
+
+            @pl.when(turn == when)
+            def _(when=when):
+                finish_tile(2 * when + 1)
 
         return carry
 
     lax.fori_loop(0, 2, two_tiles, 0)
-    scores(rest, REST, TILES - 1, s1, m1)
-    absorb(rest, REST, TILES - 2, s0, m0)
-    finish_block(2)
-    absorb(rest, REST, TILES - 1, s1, m1)
-    finish_block(3)
+    scores(*rest, TILES - 1, s1, m1)
+    absorb(*rest, TILES - 2, s0, m0)
+    finish_tile(TILES - 2)
+    absorb(*rest, TILES - 1, s1, m1)
+    finish_tile(TILES - 1)
 
     def result_copy(e):
         return pltpu.make_async_remote_copy(
@@ -386,8 +441,12 @@
 
     @pl.when(home)
     def _():
-        for e in range(1, NY):
+        for e in NEAR + FAR:
             row_copy(e).wait_send()
+
+    @pl.when(jnp.logical_not(home))
+    def _():
+        last_row_copy().wait_send()
 
     @pl.when(owner)
     def _():
@@ -440,6 +499,7 @@
             dma((1,)),
             pltpu.SemaphoreType.REGULAR,
             pltpu.SemaphoreType.REGULAR,
+            pltpu.SemaphoreType.REGULAR,
         ],
         compiler_params=pltpu.CompilerParams(
             collective_id=0, has_side_effects=True, vmem_limit_bytes=63 * 2**20

time: 44.4 us -> 41.1 us (0.926)
  Pallas kernels: 43.6 us -> 40.2 us
    pallas_call x1, Pallas kernels: 42.1 us -> 38.8 us  [on_device(): pl.pallas_call(kernel, out_shape=shapes, in_specs=[pl.BlockSpec(memory_sp...]
where the time goes in v4:
time: 41.1 us; the launch traced here: 40.9 us
  Pallas kernels  40.2 us (98%)
  between operations  0.64 us (2%)
    pallas_call x1, Pallas kernels, on_device(): pl.pallas_call(kernel, out_shape=shapes, in_specs=[pl.BlockSpec(memory_sp...  38.8 us
    pallas_call x1, Pallas kernels, on_device(): pl.pallas_call(hand_over, out_shape=shapes, in_specs=[pl.BlockSpec(memory...  1.43 us

profile of v4, /device:TPU:1, one launch (start us, length us, event | category | flops | bytes accessed | tf_op | source)
XLA Modules:
  0.0 40.9 jit_solution(14973115498743813994)
XLA Ops:
  0.6 38.8 %shard_map.68 = (f32[384]{0:T(512)}, f32[32,384]{1,0:T(8,128)}) custom-call(f32[32,384]{1,0:T(8,128)} %x_hbm.1, f32[384]{0:T(512)} %w_hbm.1, f32[32,256]{1,0:T(8,128)} %y_hbm.1, f32[1,256]{1,0:T(1,128)} %g_hbm.1, f32[1,256]{1,0:T(1,128)} %l_hbm.1), custom_call_target="tpu_custom_call" | custom-call | tf_op jit(solution)/shard_map/pallas_call | solution.py:465
  39.5 1.4 %shard_map.69 = (f32[384]{0:T(512)}, f32[32,384]{1,0:T(8,128)}) custom-call(f32[384]{0:T(512)} %get-tuple-element.4.pot_in, f32[32,384]{1,0:T(8,128)} %get-tuple-element.5.bary_in), custom_call_target="tpu_custom_call" | custom-call | tf_op jit(solution)/shard_map/pallas_call | solution.py:508

commit v5 on v4

--- a/solution.py
+++ b/solution.py
@@ -17,19 +17,17 @@
 NY, NZ, NX, CORES = 8, 8, 4, 2
 DIMS, ROWS, COLS = 32, 384, 256
 TILE = 256
-GROUP = 4
 SHARDS = NZ * CORES
 BLOCKS = NY // CORES
-SPAN = GROUP * COLS
 TILES = BLOCKS * ROWS // TILE
-REST = SHARDS * COLS - 2 * SPAN
 DEPTH = 256
 LANES = 128
 COL_TALL = 72
 PIECE_TALL = 40
 OWNERS = ROWS // LANES
 
-COLUMNS = (0, 8, 1, 2, 9, 10, 3, 11, 4, 12, 5, 13, 6, 14, 7, 15)
+COLUMNS = (0, 8, 1, 2, 9, 10, 3, 11, 7, 6, 5, 4, 15, 14, 13, 12)
+GROUPS = (4, 3, 5, 4)
 SPOT = {place: spot for spot, place in enumerate(COLUMNS)}
 LOW = 4
 
@@ -51,14 +49,21 @@
 def kernel(
     x_hbm, w_hbm, y_hbm, g_hbm, l_hbm, pot_ref, bary_ref,
     xown, wown, yown, gown, lown, xraw, craw, ya, yw, xa, s0, s1, m0, m1, mrun, acc, pout, pin, fin,
-    in_sem, crecv, csend, fsend, rrecv, rsend, precv, psend, frecv, tsend, ready, ready_two, later_in,
+    in_sem, crecv, csend, fsend, rrecv, rsend, precv, psend, frecv, tsend, ready, ready_two, later_in, aside,
 ):
+    loads = [
+        pltpu.make_async_copy(a, b, in_sem.at[i])
+        for i, (a, b) in enumerate(((x_hbm, xown), (y_hbm, yown), (g_hbm, gown), (l_hbm, lown), (w_hbm, wown)))
+    ]
+    for load in loads:
+        load.start()
     src, tgt = lax.axis_index("src"), lax.axis_index("tgt")
     yi, zi = src // NZ, src % NZ
     xi, core = tgt // CORES, tgt % CORES
     odd = (yi + core) % 2
     home = odd == 0
     low = zi < LOW
+    high = jnp.logical_not(low)
     owner = jnp.logical_and(core == 1, xi < OWNERS)
 
     def y_peer(e):
@@ -79,35 +84,33 @@
 
     barrier = pltpu.get_barrier_semaphore()
 
-    def greet(device):
-        pl.semaphore_signal(barrier, inc=1, device_id=device, device_id_type=MESH)
+    ear = jnp.where(low, core, 1)
+
+    def greet(device, at):
+        where, chip_core = device
+        there = (where, (chip_core // CORES) * CORES + at)
+        pl.semaphore_signal(barrier, inc=1, device_id=there, device_id_type=MESH)
 
     @pl.when(low)
     def _():
         for tie in range(LOW, NZ):
-            greet(z_peer(tie))
+            greet(z_peer(tie), 0)
 
     for tie in (3, 2, 1):
-        greet(z_peer(tie))
+        greet(z_peer(tie), ear)
     for e in reversed(NEAR + FAR):
         if e % 2:
-            greet(y_peer(e))
+            greet(y_peer(e), ear)
         else:
 
             @pl.when(home)
             def _(e=e):
-                greet(y_peer(e))
+                greet(y_peer(e), ear)
 
     for e in (1, NX - 1):
-        greet(x_peer(e))
-    greet(sibling)
-
-    loads = [
-        pltpu.make_async_copy(a, b, in_sem.at[i])
-        for i, (a, b) in enumerate(((x_hbm, xown), (y_hbm, yown), (g_hbm, gown), (l_hbm, lown), (w_hbm, wown)))
-    ]
-    for load in loads:
-        load.start()
+        greet(x_peer(e), ear)
+    greet(sibling, 1 - core)
+
     mrun[...] = jnp.full_like(mrun, -1e30)
     acc[...] = jnp.zeros_like(acc)
     for load in loads:
@@ -126,7 +129,13 @@
     def _():
         xraw[3] = xown[...]
 
-    pl.semaphore_wait(barrier, 16 - 2 * odd - 4 * jnp.where(low, 1, 0))
+    @pl.when(low)
+    def _():
+        pl.semaphore_wait(barrier, 12 - 2 * odd)
+
+    @pl.when(jnp.logical_and(high, core == 0))
+    def _():
+        pl.semaphore_wait(barrier, 9)
 
     def column_copy(tie):
         return pltpu.make_async_remote_copy(
@@ -272,16 +281,35 @@
         wait_rows(slot)
         prepare_rows(slot)
 
+    def tell_sibling():
+        pl.semaphore_signal(aside, inc=1, device_id=sibling, device_id_type=MESH)
+
+    @pl.when(jnp.logical_and(high, core == 0))
+    def _():
+        tell_sibling()
+
+    @pl.when(jnp.logical_and(high, core == 1))
+    def _():
+        pl.semaphore_wait(aside, 1)
+
+    @pl.when(high)
+    def _():
+        across()
+        for tie in range(LOW, NZ):
+            pl.semaphore_signal(later_in, inc=1, device_id=z_peer(tie), device_id_type=MESH)
+
+    @pl.when(jnp.logical_and(high, core == 1))
+    def _():
+        pl.semaphore_wait(barrier, 21)
+        tell_sibling()
+
+    @pl.when(jnp.logical_and(high, core == 0))
+    def _():
+        pl.semaphore_wait(aside, 1)
+
     pass_copy(0).start()
     column_copy(1).start()
     send_rows(NEAR)
-
-    @pl.when(jnp.logical_not(low))
-    def _():
-        across()
-        for tie in range(LOW, NZ):
-            pl.semaphore_signal(later_in, inc=1, device_id=z_peer(tie), device_id_type=MESH)
-
     column_copy(2).start()
     prepare(0)
 
@@ -308,12 +336,11 @@
         if done is not None:
             absorb(*done, *buffers[number % 2])
 
-    one, two, rest = (0, SPAN), (SPAN, SPAN), (2 * SPAN, REST)
+    one, two, three, rest = ((COLS * sum(GROUPS[:i]), COLS * GROUPS[i]) for i in range(4))
 
     step(-1, None, (*one, 5))
     take_rows(2)
     step(0, (*one, 5), (*one, 4))
-    take(3)
     step(1, (*one, 4), (*one, 3))
     take_rows(1)
 
@@ -323,15 +350,16 @@
         last_row_copy().start()
         prepare_rows(0)
 
-    step(2, (*one, 3), (*one, 2))
-    arrived(1, 2, 3)
-    prepare(9, 10, 3, 11)
-    step(3, (*one, 2), (*two, 5))
-
     @pl.when(low)
     def _():
         pl.semaphore_wait(later_in, NZ - LOW)
         across()
+
+    step(2, (*one, 3), (*one, 2))
+    arrived(1, 2)
+    take(3)
+    prepare(9, 10, 3)
+    step(3, (*one, 2), (*two, 5))
 
     step(4, (*two, 5), (*two, 4))
     step(5, (*two, 4), (*two, 3))
@@ -345,45 +373,37 @@
         pl.semaphore_signal(ready, inc=1, device_id=x_peer(e), device_id_type=MESH)
     step(7, (*two, 2), (*one, 1))
     step(8, (*one, 1), (*one, 0))
+    step(9, (*one, 0), (*two, 1))
+    step(10, (*two, 1), (*two, 0))
     take(7, 6, 5, 4)
-    prepare(7, 6, 5, 4)
-    step(9, (*one, 0), (*two, 1))
+    arrived(3)
+    prepare(11, 7, 6, 5, 4)
+    step(11, (*two, 0), (*three, 0))
     pl.semaphore_wait(ready, 2)
     for e in (1, NX - 1):
         pl.semaphore_signal(ready_two, inc=1, device_id=x_peer(e), device_id_type=MESH)
-    step(10, (*two, 1), (*two, 0))
+    step(12, (*three, 0), (*three, 1))
+    step(13, (*three, 1), (*three, 2))
     arrived(7, 6, 5, 4)
     prepare(15, 14, 13, 12)
-
-    step(11, (*two, 0), (*rest, 0))
-
-    def two_tiles(turn, carry):
-        scores(*rest, 2 * turn + 1, s1, m1)
-        absorb(*rest, 2 * turn, s0, m0)
-        for when in range(2):
-
-            @pl.when(turn == when)
-            def _(when=when):
-                if when == 0:
-                    pl.semaphore_wait(ready_two, 2)
-                finish_tile(2 * when)
-
-        scores(*rest, 2 * turn + 2, s0, m0)
-        absorb(*rest, 2 * turn + 1, s1, m1)
-        for when in range(2):
-
-            @pl.when(turn == when)
-            def _(when=when):
-                finish_tile(2 * when + 1)
-
-        return carry
-
-    lax.fori_loop(0, 2, two_tiles, 0)
-    scores(*rest, TILES - 1, s1, m1)
-    absorb(*rest, TILES - 2, s0, m0)
-    finish_tile(TILES - 2)
-    absorb(*rest, TILES - 1, s1, m1)
-    finish_tile(TILES - 1)
+    step(14, (*three, 2), (*rest, 0))
+
+    step(15, (*rest, 0), (*three, 3))
+    pl.semaphore_wait(ready_two, 2)
+    finish_tile(0)
+    step(16, (*three, 3), (*rest, 1))
+    step(17, (*rest, 1), (*three, 4))
+    finish_tile(1)
+    step(18, (*three, 4), (*rest, 2))
+    step(19, (*rest, 2), (*three, 5))
+    finish_tile(2)
+    step(20, (*three, 5), (*rest, 3))
+    step(21, (*rest, 3), (*rest, 4))
+    finish_tile(3)
+    step(22, (*rest, 4), (*rest, 5))
+    finish_tile(4)
+    step(23, (*rest, 5), None)
+    finish_tile(5)
 
     def result_copy(e):
         return pltpu.make_async_remote_copy(
@@ -478,8 +498,8 @@
             vmem((SHARDS * COLS, DEPTH), BF16),
             vmem((80, SHARDS * COLS), BF16),
             vmem((DEPTH, BLOCKS * ROWS), BF16),
-            vmem((REST, TILE), F32),
-            vmem((REST, TILE), F32),
+            vmem((COLS * max(GROUPS), TILE), F32),
+            vmem((COLS * max(GROUPS), TILE), F32),
             vmem((8, TILE), F32),
             vmem((8, TILE), F32),
             vmem((8, BLOCKS * ROWS), F32),
@@ -500,6 +520,7 @@
             pltpu.SemaphoreType.REGULAR,
             pltpu.SemaphoreType.REGULAR,
             pltpu.SemaphoreType.REGULAR,
+            pltpu.SemaphoreType.REGULAR,
         ],
         compiler_params=pltpu.CompilerParams(
             collective_id=0, has_side_effects=True, vmem_limit_bytes=63 * 2**20

time: 41.1 us -> 40.7 us (level)
    pallas_call x1, Pallas kernels: 38.8 us -> 38.4 us  [on_device(): pl.pallas_call(kernel, out_shape=shapes, in_specs=[pl.BlockSpec(memory_sp...]
where the time goes in v5:
time: 40.7 us; the launch traced here: 40.4 us
  Pallas kernels  39.8 us (98%)
  between operations  0.64 us (2%)
    pallas_call x1, Pallas kernels, on_device(): pl.pallas_call(kernel, out_shape=shapes, in_specs=[pl.BlockSpec(memory_sp...  38.4 us
    pallas_call x1, Pallas kernels, on_device(): pl.pallas_call(hand_over, out_shape=shapes, in_specs=[pl.BlockSpec(memory...  1.43 us

profile of v5, /device:TPU:1, one launch (start us, length us, event | category | flops | bytes accessed | tf_op | source)
XLA Modules:
  0.0 40.4 jit_solution(15610567417563797322)
XLA Ops:
  0.6 38.4 %shard_map.68 = (f32[384]{0:T(512)}, f32[32,384]{1,0:T(8,128)}) custom-call(f32[32,384]{1,0:T(8,128)} %x_hbm.1, f32[384]{0:T(512)} %w_hbm.1, f32[32,256]{1,0:T(8,128)} %y_hbm.1, f32[1,256]{1,0:T(1,128)} %g_hbm.1, f32[1,256]{1,0:T(1,128)} %l_hbm.1), custom_call_target="tpu_custom_call" | custom-call | tf_op jit(solution)/shard_map/pallas_call | solution.py:485
  39.0 1.4 %shard_map.69 = (f32[384]{0:T(512)}, f32[32,384]{1,0:T(8,128)}) custom-call(f32[384]{0:T(512)} %get-tuple-element.4.pot_in, f32[32,384]{1,0:T(8,128)} %get-tuple-element.5.bary_in), custom_call_target="tpu_custom_call" | custom-call | tf_op jit(solution)/shard_map/pallas_call | solution.py:529

commit v6 on v5

--- a/solution.py
+++ b/solution.py
@@ -149,6 +149,13 @@
             recv_sem=crecv.at[NZ + tie], device_id=sibling, device_id_type=MESH,
         )
 
+    def early_copy(z):
+        tie = sum(((zi // 2**i) % 2 + (1 - 2 * ((zi // 2**i) % 2)) * (z // 2**i % 2)) * 2**i for i in range(3))
+        return pltpu.make_async_remote_copy(
+            src_ref=craw.at[0], dst_ref=craw.at[tie], send_sem=csend.at[0], recv_sem=crecv.at[tie],
+            device_id=(yi * NZ + z, tgt), device_id_type=MESH,
+        )
+
     def row_copy(e):
         back = (8 - e) % 8
         slot = EVEN.index(back) if back % 2 == 0 else ODD.index(back)
@@ -294,7 +301,8 @@
 
     @pl.when(high)
     def _():
-        across()
+        for z in range(LOW):
+            early_copy(z).start()
         for tie in range(LOW, NZ):
             pl.semaphore_signal(later_in, inc=1, device_id=z_peer(tie), device_id_type=MESH)
 

time: 40.7 us -> 40.1 us (0.985)
  Pallas kernels: 39.8 us -> 39.3 us
    pallas_call x1, Pallas kernels: 38.4 us -> 37.8 us  [on_device(): pl.pallas_call(kernel, out_shape=shapes, in_specs=[pl.BlockSpec(memory_sp...]
where the time goes in v6:
time: 40.1 us; the launch traced here: 39.9 us
  Pallas kernels  39.3 us (98%)
  between operations  0.64 us (2%)
    pallas_call x1, Pallas kernels, on_device(): pl.pallas_call(kernel, out_shape=shapes, in_specs=[pl.BlockSpec(memory_sp...  37.8 us
    pallas_call x1, Pallas kernels, on_device(): pl.pallas_call(hand_over, out_shape=shapes, in_specs=[pl.BlockSpec(memory...  1.43 us

profile of v6, /device:TPU:1, one launch (start us, length us, event | category | flops | bytes accessed | tf_op | source)
XLA Modules:
  0.0 39.9 jit_solution(5884084616574173481)
XLA Ops:
  0.6 37.8 %shard_map.68 = (f32[384]{0:T(512)}, f32[32,384]{1,0:T(8,128)}) custom-call(f32[32,384]{1,0:T(8,128)} %x_hbm.1, f32[384]{0:T(512)} %w_hbm.1, f32[32,256]{1,0:T(8,128)} %y_hbm.1, f32[1,256]{1,0:T(1,128)} %g_hbm.1, f32[1,256]{1,0:T(1,128)} %l_hbm.1), custom_call_target="tpu_custom_call" | custom-call | tf_op jit(solution)/shard_map/pallas_call | solution.py:493
  38.5 1.4 %shard_map.69 = (f32[384]{0:T(512)}, f32[32,384]{1,0:T(8,128)}) custom-call(f32[384]{0:T(512)} %get-tuple-element.4.pot_in, f32[32,384]{1,0:T(8,128)} %get-tuple-element.5.bary_in), custom_call_target="tpu_custom_call" | custom-call | tf_op jit(solution)/shard_map/pallas_call | solution.py:537
